TPU v7x, 32 devices: a whole 2x2x4 slice. The times are simulated.
32 devices in a mesh: seq: 4 (over y, x), head: 8 (over z, core).
Axes of the slice: x: 2, y: 2, z: 4, core: 2. Of those that a mesh axis runs over, the one named last changes fastest.
Arguments:
- signal: bfloat16 [8192, 5120], P('seq', 'head'), may hold values from -0.119628906 to 0.119628906
- log_decay: float32 [80, 8192], P('head', 'seq'), may hold values from -0.6 to 0
- b_matrix: bfloat16 [8192, 128], P('seq'), may hold values from -6 to 6
- c_matrix: bfloat16 [8192, 128], P('seq'), may hold values from -0.5 to 0.5
- out_grad: bfloat16 [8192, 5120], P('seq', 'head'), may hold values from -0.4 to 0.4
Outputs:
- output: float32 [8192, 5120], P('seq', 'head')
- grad_signal: float32 [8192, 5120], P('seq', 'head')
- grad_decay: float32 [80, 8192], P('head', 'seq')
- grad_b: float32 [8192, 128], P(('seq', 'head'))
- grad_c: float32 [8192, 128], P(('seq', 'head'))
- head_grads: float32 [2, 80], P(None, 'head')
All inputs are finite; a program needn't handle non-finite values.
Results may differ from a plain program's by a relative error of at most 0.012.
Values sent between devices are 32-bit elements; how exact they have to be, the bound alone decides.
A program may use at most 192 MiB of HBM per device.

v0:
```python
import jax
import jax.numpy as jnp
from jax import lax
from jax.sharding import PartitionSpec as P

SPAN = 256


highest = lax.Precision.HIGHEST


def carried_in(value, axis, join, neutral, backward):
    count, mine = (lax.axis_size(axis), lax.axis_index(axis))
    pieces = jax.tree.map(lambda part: lax.all_gather(part, axis), value)
    if backward:
        pieces = jax.tree.map(lambda part: part[::-1], pieces)
        mine = count - 1 - mine
    so_far = jax.tree.map(
        lambda part, zero: jnp.full_like(part, 0) + jnp.asarray(zero, part.dtype), value, neutral
    )

    def hop(position, so_far):
        longer = join(so_far, jax.tree.map(lambda part: part[position], pieces))
        return jax.tree.map(lambda new, old: jnp.where(position < mine, new, old), longer, so_far)

    return lax.fori_loop(0, count - 1, hop, so_far)


def span_step(state, inputs):
    values, decays, b_block, c_block = inputs
    cumulated = jnp.cumsum(decays, axis=1)
    length = decays.shape[1]
    lower = jnp.tril(jnp.ones((length, length), dtype=bool))
    spread = cumulated[:, :, None] - cumulated[:, None, :]
    weights = jnp.where(lower[None], jnp.exp(jnp.where(lower[None], spread, 0.0)), 0.0)
    b_half = b_block.astype(jnp.bfloat16)
    c_half = c_block.astype(jnp.bfloat16)
    scores = jnp.dot(c_half, b_half.T, preferred_element_type=jnp.float32)
    mixing = (weights * scores[None]).astype(jnp.bfloat16)
    inner = jnp.einsum(
        "hij,jhp->ihp", mixing, values.astype(jnp.bfloat16), preferred_element_type=jnp.float32
    )
    carried = (
        jnp.einsum("in,hpn->ihp", c_block, state, precision=highest)
        * jnp.exp(cumulated).T[:, :, None]
    )
    last_sum = cumulated[:, -1]
    tails = jnp.exp(last_sum[:, None] - cumulated)
    scaled = (values * tails.T[:, :, None]).astype(jnp.bfloat16)
    update = jnp.einsum("jhp,jn->hpn", scaled, b_half, preferred_element_type=jnp.float32)
    state = jnp.exp(last_sum)[:, None, None] * state + update
    return (state, inner + carried)


def slab_core(values, decays, b_full, c_full):
    length, heads, width = values.shape
    blocks = length // SPAN
    stacked = values.reshape(blocks, SPAN, heads, width)
    decay_blocks = decays.reshape(heads, blocks, SPAN).transpose(1, 0, 2)
    b_blocks = b_full.reshape(blocks, SPAN, b_full.shape[1])
    c_blocks = c_full.reshape(blocks, SPAN, c_full.shape[1])
    start = jnp.zeros((heads, width, b_full.shape[1]), jnp.float32)
    final_state, outputs = lax.scan(span_step, start, (stacked, decay_blocks, b_blocks, c_blocks))
    return (outputs.reshape(length, heads, width), final_state)


def attach_entry(decays, c_full, inner, local_state, entry):
    cumulated = jnp.cumsum(decays, axis=1)
    carried = (
        jnp.einsum("tn,hpn->thp", c_full, entry, precision=highest)
        * jnp.exp(cumulated).T[:, :, None]
    )
    leaving = jnp.exp(cumulated[:, -1])[:, None, None] * entry + local_state
    return (inner + carried, leaving)


def linked(earlier, later):
    return (earlier[0] * later[0], later[0][:, None, None] * earlier[1] + later[1])


def shards(signal, log_decay, b_matrix, c_matrix, out_grad):
    length = signal.shape[0]
    heads = log_decay.shape[0]
    width = signal.shape[1] // heads
    values = signal.astype(jnp.float32).reshape(length, heads, width)
    b_full = b_matrix.astype(jnp.float32)
    c_full = c_matrix.astype(jnp.float32)
    (inner, local_state), pull_core = jax.vjp(slab_core, values, log_decay, b_full, c_full)
    totals = jnp.sum(log_decay, axis=1)
    factor = jnp.exp(totals)
    identity = (jnp.ones_like(factor), jnp.zeros_like(local_state))
    entry = carried_in((factor, local_state), "seq", linked, identity, False)[1]

    def attach_fixed(decays, c_used, inner_part, state_part):
        return attach_entry(decays, c_used, inner_part, state_part, entry)

    (mixed, leaving), pull_attach = jax.vjp(attach_fixed, log_decay, c_full, inner, local_state)
    grad_out = out_grad.astype(jnp.float32).reshape(length, heads, width)
    cumulated = jnp.cumsum(log_decay, axis=1)
    weighted = grad_out * jnp.exp(cumulated).T[:, :, None]
    own_adjoint = jnp.einsum("thp,tn->hpn", weighted, c_full, precision=highest)
    after = carried_in((factor, own_adjoint), "seq", linked, identity, True)[1]
    decay_part, c_part, inner_grad, state_grad = pull_attach((grad_out, after))
    value_grad, decay_core, b_grad, c_core = pull_core((inner_grad, state_grad))
    value_grad = value_grad + grad_out
    grad_decay = decay_part + decay_core
    c_grad = c_part + c_core
    grad_b, grad_c = (
        lax.psum_scatter(b_grad, "head", scatter_dimension=0, tiled=True),
        lax.psum_scatter(c_grad, "head", scatter_dimension=0, tiled=True),
    )
    local_params = jnp.stack(
        [jnp.sum(grad_out * values, axis=(0, 2)), jnp.sum(grad_decay * log_decay, axis=1)]
    )
    head_grads = lax.psum(local_params, "seq")
    output = (mixed + values).reshape(length, heads * width)
    grad_signal = value_grad.reshape(length, heads * width)
    return (output, grad_signal, grad_decay, grad_b, grad_c, head_grads)


def solution(mesh):
    in_specs = (
        P("seq", "head"),
        P("head", "seq"),
        P("seq", None),
        P("seq", None),
        P("seq", "head"),
    )
    out_specs = (
        P("seq", "head"),
        P("seq", "head"),
        P("head", "seq"),
        P(("seq", "head"), None),
        P(("seq", "head"), None),
        P(None, "head"),
    )
    return jax.shard_map(shards, mesh=mesh, in_specs=in_specs, out_specs=out_specs, check_vma=False)
```

profile of v0, /device:TPU:0, one launch (start us, length us, event | category | flops | bytes accessed | tf_op | source)
XLA Modules:
  0.0 814.6 jit_solution(16520793237982977648)
XLA Ops:
  15.0 3.9 copy.135
  23.2 275.8 %while.106 = (s32[]{:T(128)}, f32[10,64,128]{2,1,0:T(8,128)S(1)}, f32[8,256,10,64]{1,0,3,2:T(8,128)}, f32[8,10,256,256]{3,2,1,0:T(8,128)}, bf16[8,128,256]{1,2,0...) while((s32[]{:T(128)}, f32[10,64,128]{2,1,0:T(8,128)S(1)}, ...), condition=%wide.region_3.4_spmd.clone.clone, body=%wide.region_0.3_spmd.clone.clone.sunk | while | flops 404512288 | bytes 18531628 | solution.py:63
  31.0 15.6 %dynamic_update_slice.256 = f32[8,256,10,64]{1,0,3,2:T(8,128)} dynamic-update-slice(f32[8,256,10,64]{1,0,3,2:T(8,128)} %get-tuple-element.2359, f32[1,256,10,64]{1,0,3,2:T(1,128)S(1)} %copy.232, s32[]{:T(128)} %get-tuple-element.2357, s32[]{:T(128)} %constant.220.clone.1..sunk.3, s32[]{:T(128)} %constant.220.clone.1..sunk.3, s32[]{:T(128)} %constant.220.clone.1..sunk.3) | dynamic-update-slice | bytes 1310724 | tf_op jit(solution)/shard_map/jvp()/while/body/jit(dynamic_update_index_in_dim)/dynamic_update_slice | solution.py:63
  65.5 15.6 %dynamic_update_slice.256 = f32[8,256,10,64]{1,0,3,2:T(8,128)} dynamic-update-slice(f32[8,256,10,64]{1,0,3,2:T(8,128)} %get-tuple-element.2359, f32[1,256,10,64]{1,0,3,2:T(1,128)S(1)} %copy.232, s32[]{:T(128)} %get-tuple-element.2357, s32[]{:T(128)} %constant.220.clone.1..sunk.3, s32[]{:T(128)} %constant.220.clone.1..sunk.3, s32[]{:T(128)} %constant.220.clone.1..sunk.3) | dynamic-update-slice | bytes 1310724 | tf_op jit(solution)/shard_map/jvp()/while/body/jit(dynamic_update_index_in_dim)/dynamic_update_slice | solution.py:63
  100.1 15.6 %dynamic_update_slice.256 = f32[8,256,10,64]{1,0,3,2:T(8,128)} dynamic-update-slice(f32[8,256,10,64]{1,0,3,2:T(8,128)} %get-tuple-element.2359, f32[1,256,10,64]{1,0,3,2:T(1,128)S(1)} %copy.232, s32[]{:T(128)} %get-tuple-element.2357, s32[]{:T(128)} %constant.220.clone.1..sunk.3, s32[]{:T(128)} %constant.220.clone.1..sunk.3, s32[]{:T(128)} %constant.220.clone.1..sunk.3) | dynamic-update-slice | bytes 1310724 | tf_op jit(solution)/shard_map/jvp()/while/body/jit(dynamic_update_index_in_dim)/dynamic_update_slice | solution.py:63
  134.6 15.6 %dynamic_update_slice.256 = f32[8,256,10,64]{1,0,3,2:T(8,128)} dynamic-update-slice(f32[8,256,10,64]{1,0,3,2:T(8,128)} %get-tuple-element.2359, f32[1,256,10,64]{1,0,3,2:T(1,128)S(1)} %copy.232, s32[]{:T(128)} %get-tuple-element.2357, s32[]{:T(128)} %constant.220.clone.1..sunk.3, s32[]{:T(128)} %constant.220.clone.1..sunk.3, s32[]{:T(128)} %constant.220.clone.1..sunk.3) | dynamic-update-slice | bytes 1310724 | tf_op jit(solution)/shard_map/jvp()/while/body/jit(dynamic_update_index_in_dim)/dynamic_update_slice | solution.py:63
  169.1 15.6 %dynamic_update_slice.256 = f32[8,256,10,64]{1,0,3,2:T(8,128)} dynamic-update-slice(f32[8,256,10,64]{1,0,3,2:T(8,128)} %get-tuple-element.2359, f32[1,256,10,64]{1,0,3,2:T(1,128)S(1)} %copy.232, s32[]{:T(128)} %get-tuple-element.2357, s32[]{:T(128)} %constant.220.clone.1..sunk.3, s32[]{:T(128)} %constant.220.clone.1..sunk.3, s32[]{:T(128)} %constant.220.clone.1..sunk.3) | dynamic-update-slice | bytes 1310724 | tf_op jit(solution)/shard_map/jvp()/while/body/jit(dynamic_update_index_in_dim)/dynamic_update_slice | solution.py:63
  203.5 15.6 %dynamic_update_slice.256 = f32[8,256,10,64]{1,0,3,2:T(8,128)} dynamic-update-slice(f32[8,256,10,64]{1,0,3,2:T(8,128)} %get-tuple-element.2359, f32[1,256,10,64]{1,0,3,2:T(1,128)S(1)} %copy.232, s32[]{:T(128)} %get-tuple-element.2357, s32[]{:T(128)} %constant.220.clone.1..sunk.3, s32[]{:T(128)} %constant.220.clone.1..sunk.3, s32[]{:T(128)} %constant.220.clone.1..sunk.3) | dynamic-update-slice | bytes 1310724 | tf_op jit(solution)/shard_map/jvp()/while/body/jit(dynamic_update_index_in_dim)/dynamic_update_slice | solution.py:63
  237.9 15.6 %dynamic_update_slice.256 = f32[8,256,10,64]{1,0,3,2:T(8,128)} dynamic-update-slice(f32[8,256,10,64]{1,0,3,2:T(8,128)} %get-tuple-element.2359, f32[1,256,10,64]{1,0,3,2:T(1,128)S(1)} %copy.232, s32[]{:T(128)} %get-tuple-element.2357, s32[]{:T(128)} %constant.220.clone.1..sunk.3, s32[]{:T(128)} %constant.220.clone.1..sunk.3, s32[]{:T(128)} %constant.220.clone.1..sunk.3) | dynamic-update-slice | bytes 1310724 | tf_op jit(solution)/shard_map/jvp()/while/body/jit(dynamic_update_index_in_dim)/dynamic_update_slice | solution.py:63
  272.4 15.6 %dynamic_update_slice.256 = f32[8,256,10,64]{1,0,3,2:T(8,128)} dynamic-update-slice(f32[8,256,10,64]{1,0,3,2:T(8,128)} %get-tuple-element.2359, f32[1,256,10,64]{1,0,3,2:T(1,128)S(1)} %copy.232, s32[]{:T(128)} %get-tuple-element.2357, s32[]{:T(128)} %constant.220.clone.1..sunk.3, s32[]{:T(128)} %constant.220.clone.1..sunk.3, s32[]{:T(128)} %constant.220.clone.1..sunk.3) | dynamic-update-slice | bytes 1310724 | tf_op jit(solution)/shard_map/jvp()/while/body/jit(dynamic_update_index_in_dim)/dynamic_update_slice | solution.py:63
  310.9 3.3 fusion.125
  315.8 11.5 %all-reduce.2 = f32[40]{0:T(128)S(1)} all-reduce(f32[40]{0:T(128)S(1)} %exponential_dynamic-update-slice_fusion.2), channel_id=2, replica_groups=mesh['seq'=4,'head'=8] {'seq'}, use_global_device_ids=true, to_apply=%add.2 | all-reduce | flops 40 | bytes 320
  327.5 7.3 copy.173
  334.8 3.3 while.104
  338.1 24.0 %all-gather.8.cloned.1.call-done = f32[40,64,128]{2,1,0:T(8,128)} async-done(((f32[10,64,128]{2,1,0:T(8,128)}), f32[40,64,128]{2,1,0:T(8,128)}) %all-gather.8.cloned.1.call-update) | async-done | bytes 1310736 | tf_op jit(solution)/shard_map/all_gather | solution.py:14
  369.7 350.8 %while.103 = (s32[]{:T(128)}, f32[10,64,128]{2,1,0:T(8,128)S(1)}, f32[8,256,10,64]{1,0,3,2:T(8,128)}, f32[8,10,256]{2,1,0:T(8,128)}, f32[8,256,128]{2,1,0:T(8,12...) while((s32[]{:T(128)}, f32[10,64,128]{2,1,0:T(8,128)S(1)}, ...), condition=%wide.region_21.22_spmd.clone.clone, body=%wide.region_11.21_spmd.clone.clone.sunk | while | flops 796900416 | bytes 22719808 | solution.py:63
  373.2 3.0 constant_dynamic-slice_fusion.9
  377.3 3.8 fusion.196
  389.3 15.6 %dynamic_update_slice.244 = f32[8,256,10,64]{1,0,3,2:T(8,128)} dynamic-update-slice(f32[8,256,10,64]{1,0,3,2:T(8,128)} %get-tuple-element.2488, f32[1,256,10,64]{1,0,3,2:T(1,128)S(1)} %copy.220, s32[]{:T(128)S(6)} %sub.191, s32[]{:T(128)} %constant.220.clone.1..sunk, s32[]{:T(128)} %constant.220.clone.1..sunk, s32[]{:T(128)} %constant.220.clone.1..sunk) | dynamic-update-slice | bytes 1310724 | tf_op jit(solution)/shard_map/transpose(jvp())/while/body/jit(dynamic_update_index_in_dim)/dynamic_update_slice | solution.py:63
  417.1 3.0 constant_dynamic-slice_fusion.9
  421.1 3.8 fusion.196
  433.1 15.6 %dynamic_update_slice.244 = f32[8,256,10,64]{1,0,3,2:T(8,128)} dynamic-update-slice(f32[8,256,10,64]{1,0,3,2:T(8,128)} %get-tuple-element.2488, f32[1,256,10,64]{1,0,3,2:T(1,128)S(1)} %copy.220, s32[]{:T(128)S(6)} %sub.191, s32[]{:T(128)} %constant.220.clone.1..sunk, s32[]{:T(128)} %constant.220.clone.1..sunk, s32[]{:T(128)} %constant.220.clone.1..sunk) | dynamic-update-slice | bytes 1310724 | tf_op jit(solution)/shard_map/transpose(jvp())/while/body/jit(dynamic_update_index_in_dim)/dynamic_update_slice | solution.py:63
  460.9 3.0 constant_dynamic-slice_fusion.9
  465.0 3.8 fusion.196
  477.0 15.6 %dynamic_update_slice.244 = f32[8,256,10,64]{1,0,3,2:T(8,128)} dynamic-update-slice(f32[8,256,10,64]{1,0,3,2:T(8,128)} %get-tuple-element.2488, f32[1,256,10,64]{1,0,3,2:T(1,128)S(1)} %copy.220, s32[]{:T(128)S(6)} %sub.191, s32[]{:T(128)} %constant.220.clone.1..sunk, s32[]{:T(128)} %constant.220.clone.1..sunk, s32[]{:T(128)} %constant.220.clone.1..sunk) | dynamic-update-slice | bytes 1310724 | tf_op jit(solution)/shard_map/transpose(jvp())/while/body/jit(dynamic_update_index_in_dim)/dynamic_update_slice | solution.py:63
  504.8 3.0 constant_dynamic-slice_fusion.9
  508.8 3.8 fusion.196
  520.8 15.6 %dynamic_update_slice.244 = f32[8,256,10,64]{1,0,3,2:T(8,128)} dynamic-update-slice(f32[8,256,10,64]{1,0,3,2:T(8,128)} %get-tuple-element.2488, f32[1,256,10,64]{1,0,3,2:T(1,128)S(1)} %copy.220, s32[]{:T(128)S(6)} %sub.191, s32[]{:T(128)} %constant.220.clone.1..sunk, s32[]{:T(128)} %constant.220.clone.1..sunk, s32[]{:T(128)} %constant.220.clone.1..sunk) | dynamic-update-slice | bytes 1310724 | tf_op jit(solution)/shard_map/transpose(jvp())/while/body/jit(dynamic_update_index_in_dim)/dynamic_update_slice | solution.py:63
  548.6 3.0 constant_dynamic-slice_fusion.9
  552.7 3.8 fusion.196
  564.7 15.6 %dynamic_update_slice.244 = f32[8,256,10,64]{1,0,3,2:T(8,128)} dynamic-update-slice(f32[8,256,10,64]{1,0,3,2:T(8,128)} %get-tuple-element.2488, f32[1,256,10,64]{1,0,3,2:T(1,128)S(1)} %copy.220, s32[]{:T(128)S(6)} %sub.191, s32[]{:T(128)} %constant.220.clone.1..sunk, s32[]{:T(128)} %constant.220.clone.1..sunk, s32[]{:T(128)} %constant.220.clone.1..sunk) | dynamic-update-slice | bytes 1310724 | tf_op jit(solution)/shard_map/transpose(jvp())/while/body/jit(dynamic_update_index_in_dim)/dynamic_update_slice | solution.py:63
  592.5 3.0 constant_dynamic-slice_fusion.9
  596.5 3.8 fusion.196
  608.5 15.6 %dynamic_update_slice.244 = f32[8,256,10,64]{1,0,3,2:T(8,128)} dynamic-update-slice(f32[8,256,10,64]{1,0,3,2:T(8,128)} %get-tuple-element.2488, f32[1,256,10,64]{1,0,3,2:T(1,128)S(1)} %copy.220, s32[]{:T(128)S(6)} %sub.191, s32[]{:T(128)} %constant.220.clone.1..sunk, s32[]{:T(128)} %constant.220.clone.1..sunk, s32[]{:T(128)} %constant.220.clone.1..sunk) | dynamic-update-slice | bytes 1310724 | tf_op jit(solution)/shard_map/transpose(jvp())/while/body/jit(dynamic_update_index_in_dim)/dynamic_update_slice | solution.py:63
  636.3 3.0 constant_dynamic-slice_fusion.9
  640.4 3.8 fusion.196
  652.4 15.6 %dynamic_update_slice.244 = f32[8,256,10,64]{1,0,3,2:T(8,128)} dynamic-update-slice(f32[8,256,10,64]{1,0,3,2:T(8,128)} %get-tuple-element.2488, f32[1,256,10,64]{1,0,3,2:T(1,128)S(1)} %copy.220, s32[]{:T(128)S(6)} %sub.191, s32[]{:T(128)} %constant.220.clone.1..sunk, s32[]{:T(128)} %constant.220.clone.1..sunk, s32[]{:T(128)} %constant.220.clone.1..sunk) | dynamic-update-slice | bytes 1310724 | tf_op jit(solution)/shard_map/transpose(jvp())/while/body/jit(dynamic_update_index_in_dim)/dynamic_update_slice | solution.py:63
  684.2 3.8 fusion.196
  696.2 15.6 %dynamic_update_slice.244 = f32[8,256,10,64]{1,0,3,2:T(8,128)} dynamic-update-slice(f32[8,256,10,64]{1,0,3,2:T(8,128)} %get-tuple-element.2488, f32[1,256,10,64]{1,0,3,2:T(1,128)S(1)} %copy.220, s32[]{:T(128)S(6)} %sub.191, s32[]{:T(128)} %constant.220.clone.1..sunk, s32[]{:T(128)} %constant.220.clone.1..sunk, s32[]{:T(128)} %constant.220.clone.1..sunk) | dynamic-update-slice | bytes 1310724 | tf_op jit(solution)/shard_map/transpose(jvp())/while/body/jit(dynamic_update_index_in_dim)/dynamic_update_slice | solution.py:63
  720.5 21.7 %fusion.132 = f32[2048,128]{1,0:T(8,128)} fusion(f32[2048,128]{1,0:T(8,128)} %bitcast.462, f32[10,64,128]{2,1,0:T(8,128)S(1)} %get-tuple-element.1080, f32[2048,10,64]{0,2,1:T(8,128)} %bitcast.444, f32[2048,10]{0,1:T(8,128)S(1)} %exponential_bitcast_fusion.1), kind=kOutput, calls=%fused_computation.176 | convolution fusion | flops 2014838784 | bytes 7749632 | tf_op jit(solution)/shard_map/transpose(jvp(tn,hpn->thp))/dot_general | solution.py:70
  742.2 6.8 reshape.461
  749.0 10.9 %fusion.122 = (f32[2048,10]{0,1:T(8,128)S(1)}, f32[2048,10,64]{0,2,1:T(8,128)}) fusion(f32[2048,10,64]{0,2,1:T(8,128)} %bitcast.445, f32[2048,10,64]{0,2,1:T(8,128)} %bitcast.447, f32[2048,10,64]{0,2,1:T(8,128)} %reshape.461, f32[2048,10]{0,1:T(8,128)S(1)} %exponential_bitcast_fusion.1, f32[10,64,128]{2,1,0:T(8,128)S(1)} %get-tuple-element.1080, ...), kind=kOutput, calls=%fused_computation.166 | convolution fusion | flops 2019799040 | bytes 21987328 | tf_op jit(solution)/shard_map/jvp(tn,hpn->thp)/dot_general | solution.py:70
  760.5 12.4 %reduce-window.58 = f32[10,16,128]{2,1,0:T(8,128)S(1)} reduce-window(f32[10,16,128]{2,1,0:T(8,128)S(1)} %slice.74, f32[]{:T(128)} %constant.221.clone.1), window={size=1x1x128 pad=0_0x0_0x0_127}, to_apply=%region_24.25 | reduce-window | flops 2600960 | bytes 163844 | tf_op jit(solution)/shard_map/reduce-window.2
  773.6 5.2 copy.174
  778.8 4.1 multiply_reduce_fusion
  783.9 9.5 %psum.7 = f32[2,10]{1,0:T(2,128)} all-reduce(f32[2,10]{1,0:T(2,128)S(1)} %pad_maximum_fusion), channel_id=1, replica_groups=mesh['seq'=4,'head'=8] {'seq'}, use_global_device_ids=true, to_apply=%region_31.32 | all-reduce | flops 20 | bytes 160 | tf_op jit(solution)/shard_map/psum | solution.py:115
  793.4 5.9 copy.147
  799.3 5.9 copy.146
  (615 shorter events, 364.4 us)
Async XLA Ops:
  7.2 327.6 %all-gather.6.cloned.1.call-start = ((), (), s32[]{:S(2)}) async-start(), calls=%async_computation.4 | async-start | bytes 1638400 | tf_op jit(solution)/shard_map/all_gather | solution.py:14
  10.4 1.7 copy-start.3
  12.1 2.9 copy-start.2
  15.0 3.9 copy-start.8
  15.0 4.0 copy-start.10
  299.0 0.7 copy-start.1
  299.0 4.4 copy-start.7
  299.7 62.4 %all-gather.8.cloned.1.call-start = ((), (), s32[]{:S(2)}) async-start(), calls=%async_computation.5 | async-start | bytes 1638400 | tf_op jit(solution)/shard_map/all_gather | solution.py:14
  307.1 1.5 copy-start.5
  307.1 1.5 copy-start.12
  308.6 2.4 copy-start
  310.9 3.5 copy-start.15
  314.2 490.9 %reduce-scatter.5.cloned.1.call-start = ((), (), s32[]{:S(2)}) async-start(), calls=%async_computation.3 | async-start | bytes 1179648 | tf_op jit(solution)/shard_map/reduce_scatter | solution.py:110
  742.2 65.7 %reduce-scatter.3.cloned.1.call-start = ((), (), s32[]{:S(2)}) async-start(), calls=%async_computation.2 | async-start | bytes 1179648 | tf_op jit(solution)/shard_map/reduce_scatter | solution.py:109
  742.2 6.8 copy-start.9
  749.0 11.2 %copy-start.13 = (f32[2,8,16,128]{3,1,2,0:T(8,128)S(1)}, f32[2,8,16,128]{3,1,2,0:T(8,128)}, u32[]{:S(2)}) copy-start(f32[2,8,16,128]{3,1,2,0:T(8,128)} %copy.172) | copy-start | bytes 393220
  760.0 13.4 %copy-start.14 = (f32[8,10,256]{2,1,0:T(8,128)S(1)}, f32[8,10,256]{2,1,0:T(8,128)}, u32[]{:S(2)}) copy-start(f32[8,10,256]{2,1,0:T(8,128)} %get-tuple-element.1100) | copy-start | bytes 245764
  773.5 5.2 copy-start.4
  773.6 5.2 copy-start.6
  778.8 4.3 copy-start.11
Sparse Core Ops, SparseCore 0:
  299.8 31.5 all-gather.5
  333.3 28.7 all-gather.7
  742.3 32.4 reduce-scatter.4
  777.5 30.3 reduce-scatter.2
where the time goes:
time: 829 us; the launch traced here: 815 us
  local copies, waits for them, and re-layouts  400 us (48%)
  matrix products  205 us (25%)
  other arithmetic  145 us (17%)
  waiting for transfers between devices  26.8 us (3%)
  blocking collectives  21 us (3%)
  between operations  15.1 us (2%)
    dynamic_update_slice x72, local copies, waits for them, and re-layouts, slab_core(): lax.scan(span_step, start, (stacked, decay_blocks, b_blocks, c_blocks))  283 us
    dynamic_update_slice x48, other arithmetic, slab_core(): lax.scan(span_step, start, (stacked, decay_blocks, b_blocks, c_blocks))  72 us
    dot_general x24, matrix products, span_step(): jnp.einsum('hij,jhp->ihp', mixing, values.astype(jnp.bfloat16), preferred...  59.4 us
    dot_general x24, matrix products, span_step(): jnp.einsum('in,hpn->ihp', c_block, state, precision=highest)  49.1 us
    unnamed x53, local copies, waits for them, and re-layouts  43.5 us
    another operation x63, other arithmetic  42.3 us
    dot_general x24, matrix products, span_step(): jnp.einsum('jhp,jn->hpn', scaled, b_half, preferred_element_type=jnp.floa...  37.3 us
    dot_general x2, matrix products, attach_entry(): jnp.einsum('tn,hpn->thp', c_full, entry, precision=highest)  32.6 us
  transfers between devices with their start and end apart: 4, of which 2 were waited for; matrix products, arithmetic and copies ran while one was open for 9% of the time, Pallas kernels for 0%

commit v1 on v0

v1 whole, which is shorter than its diff:
```python
import functools

import jax
import jax.numpy as jnp
from jax import lax
from jax.experimental import pallas as pl
from jax.experimental.pallas import tpu as pltpu
from jax.sharding import PartitionSpec as P

SPAN = 256
F32 = jnp.float32
BF16 = jnp.bfloat16
NN = (((1,), (0,)), ((), ()))
NT = (((1,), (1,)), ((), ()))
TN = (((0,), (0,)), ((), ()))


def mm(left, right, dims):
    return lax.dot_general(left, right, dims, preferred_element_type=F32)


def sums(left, right):
    return jnp.dot(left, right, precision=lax.Precision.HIGHEST, preferred_element_type=F32)


def indices():
    rows = lax.broadcasted_iota(jnp.int32, (SPAN, SPAN), 0)
    columns = lax.broadcasted_iota(jnp.int32, (SPAN, SPAN), 1)
    return rows, columns


def states_kernel(heads, width, x_ref, dy_ref, a_ref, b_ref, c_ref,
                  xt_ref, dyt_ref, cum_ref, entry_ref, before_ref, packed_ref, sum_ref):
    k = pl.program_id(0)
    size = heads * width

    @pl.when(k == 0)
    def _():
        packed_ref[...] = jnp.zeros_like(packed_ref)
        sum_ref[...] = jnp.zeros_like(sum_ref)

    x_t = x_ref[...].astype(F32).T
    dy_t = dy_ref[...].astype(F32).T
    xt_ref[...] = x_t.astype(BF16)
    dyt_ref[...] = dy_t.astype(BF16)
    rows, columns = indices()
    cum = sums(a_ref[...], (rows <= columns).astype(F32))
    cum_ref[...] = cum
    last = cum[:, SPAN - 1:]
    head_decay = jnp.exp(cum)
    tail = jnp.exp(last - cum)
    scaled, weighted = [], []
    for h in range(heads):
        part = slice(h * width, (h + 1) * width)
        scaled.append((x_t[part] * tail[h:h + 1]).astype(BF16))
        weighted.append((dy_t[part] * head_decay[h:h + 1]).astype(BF16))
    update = mm(jnp.concatenate(scaled, axis=0), b_ref[...], NN)
    own = mm(jnp.concatenate(weighted, axis=0), c_ref[...], NN)
    before = sum_ref[...]
    before_ref[0] = jnp.exp(before)
    entry_ref[0] = packed_ref[:size]
    for h in range(heads):
        part = slice(h * width, (h + 1) * width)
        later = slice(size + h * width, size + (h + 1) * width)
        packed_ref[part] = packed_ref[part] * jnp.exp(last[h:h + 1]) + update[part]
        packed_ref[later] = packed_ref[later] + jnp.exp(before[h:h + 1]) * own[part]
    sum_ref[...] = before + last
    packed_ref[2 * size:2 * size + heads] = before + last


def core_kernel(heads, width, xt_ref, dyt_ref, a_ref, cum_ref, b_ref, c_ref,
                local_ref, before_ref, entry_ref, after_ref,
                y_ref, gx_ref, ga_ref, gbc_ref, params_ref,
                adj_ref, gs_ref, st_ref, scaled_ref, weighted_ref, yt_ref, gxt_ref):
    k = pl.program_id(0)
    state_size = b_ref.shape[1]

    @pl.when(k == 0)
    def _():
        adj_ref[...] = after_ref[...]
        params_ref[...] = jnp.zeros_like(params_ref)

    rows, columns = indices()
    lower = rows <= columns
    cum = cum_ref[...]
    last = cum[:, SPAN - 1:]
    head_decay = jnp.exp(cum)
    tail = jnp.exp(last - cum)
    whole = jnp.exp(last)
    before = before_ref[0]
    cum_columns = jnp.concatenate(
        [cum, jnp.zeros((-heads % 8, SPAN), F32)] if heads % 8 else [cum], axis=0).T
    b, c = b_ref[...], c_ref[...]
    scores = mm(b, c, NT)
    for h in range(heads):
        part = slice(h * width, (h + 1) * width)
        st_ref[part] = local_ref[0, part] + before[h:h + 1] * entry_ref[part]
    state_half = st_ref[...].astype(BF16)
    adj_half = adj_ref[...].astype(BF16)
    carried_all = mm(state_half, c, NT)
    scaled_grad_all = mm(adj_half, b, NT)
    gain, loss, skip, edge = [], [], [], []
    for h in range(heads):
        part = slice(h * width, (h + 1) * width)
        weights = jnp.where(lower, jnp.exp(cum[h:h + 1] - cum_columns[:, h:h + 1]), 0.0)
        mixing = (weights * scores).astype(BF16)
        x_half, dy_half = xt_ref[part], dyt_ref[part]
        inner = mm(x_half, mixing, NN)
        back = mm(dy_half, mixing, NT)
        mixing_grad = mm(x_half, dy_half, TN)
        piece = weights * mixing_grad
        if h == 0:
            gs_ref[...] = piece
        else:
            gs_ref[...] += piece
        x, dy = x_half.astype(F32), dy_half.astype(F32)
        core = inner + carried_all[part] * head_decay[h:h + 1]
        yt_ref[part] = core + x
        tailed = scaled_grad_all[part] * tail[h:h + 1]
        gxt_ref[part] = back + tailed + dy
        scaled_ref[part] = (x * tail[h:h + 1]).astype(BF16)
        weighted_ref[part] = (dy * head_decay[h:h + 1]).astype(BF16)
        gain.append(jnp.sum(dy * core - x * back, axis=0, keepdims=True))
        loss.append(jnp.sum(x * tailed, axis=0, keepdims=True))
        skip.append(jnp.sum(x * dy, axis=0, keepdims=True))
        products = jnp.sum(st_ref[part] * adj_ref[part], axis=0, keepdims=True)
        edge.append(jnp.sum(products, axis=1, keepdims=True))
    y_ref[...] = yt_ref[...].T
    gx_ref[...] = gxt_ref[...].T
    grad = (sums(jnp.concatenate(gain, axis=0), (rows >= columns).astype(F32))
            + sums(jnp.concatenate(loss, axis=0), (rows < columns).astype(F32))
            + whole * jnp.concatenate(edge, axis=0))
    ga_ref[...] = grad
    params_ref[0] += jnp.concatenate(skip, axis=0)
    params_ref[1] += grad * a_ref[...]
    gs_half = gs_ref[...].astype(BF16)
    gbc_ref[:, :state_size] = mm(gs_half, c, NN) + mm(scaled_ref[...], adj_half, TN)
    gbc_ref[:, state_size:] = mm(gs_half, b, TN) + mm(weighted_ref[...], state_half, TN)
    own = mm(weighted_ref[...], c, NN)
    for h in range(heads):
        part = slice(h * width, (h + 1) * width)
        adj_ref[part] = adj_ref[part] * whole[h:h + 1] + own[part]


def shards(signal, log_decay, b_matrix, c_matrix, out_grad):
    length, size = signal.shape
    heads = log_decay.shape[0]
    width = size // heads
    n = b_matrix.shape[1]
    blocks = length // SPAN
    padded = -(-(2 * size + heads) // 8) * 8
    shape = jax.ShapeDtypeStruct
    params = pltpu.CompilerParams(vmem_limit_bytes=56 * 2**20)

    token = pl.BlockSpec((SPAN, size), lambda k: (k, 0))
    flat = pl.BlockSpec((size, SPAN), lambda k: (0, k))
    decay = pl.BlockSpec((heads, SPAN), lambda k: (0, k))
    maps = pl.BlockSpec((SPAN, n), lambda k: (k, 0))
    xt, dyt, cum, local, before, packed = pl.pallas_call(
        functools.partial(states_kernel, heads, width),
        grid=(blocks,),
        in_specs=[token, token, decay, maps, maps],
        out_specs=[flat, flat, decay,
                   pl.BlockSpec((1, size, n), lambda k: (k, 0, 0)),
                   pl.BlockSpec((1, heads, n), lambda k: (k, 0, 0)),
                   pl.BlockSpec((padded, n), lambda k: (0, 0))],
        out_shape=[shape((size, length), BF16), shape((size, length), BF16),
                   shape((heads, length), F32), shape((blocks, size, n), F32),
                   shape((blocks, heads, n), F32), shape((padded, n), F32)],
        scratch_shapes=[pltpu.VMEM((heads, n), F32)],
        compiler_params=params,
    )(signal, out_grad, log_decay, b_matrix, c_matrix)

    count, mine = lax.axis_size("seq"), lax.axis_index("seq")
    pieces = lax.all_gather(packed, "seq")
    totals = pieces[:, 2 * size:2 * size + heads, 0]
    states = pieces[:, :size].reshape(count, heads, width, n)
    adjoints = pieces[:, size:2 * size].reshape(count, heads, width, n)
    place = jnp.arange(count)
    mid = place[None, :]
    ahead = (mid > place[:, None]) & (mid < mine)
    behind = (mid < place[:, None]) & (mid > mine)
    gap_in = jnp.sum(jnp.where(ahead[:, :, None], totals[None], 0.0), axis=1)
    gap_out = jnp.sum(jnp.where(behind[:, :, None], totals[None], 0.0), axis=1)
    weight_in = jnp.where((place < mine)[:, None], jnp.exp(gap_in), 0.0)
    weight_out = jnp.where((place > mine)[:, None], jnp.exp(gap_out), 0.0)
    entry = jnp.sum(weight_in[:, :, None, None] * states, axis=0).reshape(size, n)
    after = jnp.sum(weight_out[:, :, None, None] * adjoints, axis=0).reshape(size, n)

    end = blocks - 1
    token = pl.BlockSpec((SPAN, size), lambda k: (end - k, 0))
    flat = pl.BlockSpec((size, SPAN), lambda k: (0, end - k))
    decay = pl.BlockSpec((heads, SPAN), lambda k: (0, end - k))
    maps = pl.BlockSpec((SPAN, n), lambda k: (end - k, 0))
    edge = pl.BlockSpec((size, n), lambda k: (0, 0))
    y, gx, ga, gbc, sums_out = pl.pallas_call(
        functools.partial(core_kernel, heads, width),
        grid=(blocks,),
        in_specs=[flat, flat, decay, decay, maps, maps,
                  pl.BlockSpec((1, size, n), lambda k: (end - k, 0, 0)),
                  pl.BlockSpec((1, heads, n), lambda k: (end - k, 0, 0)),
                  edge, edge],
        out_specs=[token, token, decay,
                   pl.BlockSpec((SPAN, 2 * n), lambda k: (end - k, 0)),
                   pl.BlockSpec((2, heads, SPAN), lambda k: (0, 0, 0))],
        out_shape=[shape((length, size), F32), shape((length, size), F32),
                   shape((heads, length), F32), shape((length, 2 * n), F32),
                   shape((2, heads, SPAN), F32)],
        scratch_shapes=[pltpu.VMEM((size, n), F32), pltpu.VMEM((SPAN, SPAN), F32),
                        pltpu.VMEM((size, n), F32), pltpu.VMEM((size, SPAN), BF16),
                        pltpu.VMEM((size, SPAN), BF16), pltpu.VMEM((size, SPAN), F32),
                        pltpu.VMEM((size, SPAN), F32)],
        compiler_params=params,
    )(xt, dyt, log_decay, cum, b_matrix, c_matrix, local, before, entry, after)

    shared = lax.psum_scatter(gbc, "head", scatter_dimension=0, tiled=True)
    head_grads = lax.psum(jnp.sum(sums_out, axis=2), "seq")
    return y, gx, ga, shared[:, :n], shared[:, n:], head_grads


def solution(mesh):
    in_specs = (
        P("seq", "head"),
        P("head", "seq"),
        P("seq", None),
        P("seq", None),
        P("seq", "head"),
    )
    out_specs = (
        P("seq", "head"),
        P("seq", "head"),
        P("head", "seq"),
        P(("seq", "head"), None),
        P(("seq", "head"), None),
        P(None, "head"),
    )
    return jax.shard_map(shards, mesh=mesh, in_specs=in_specs, out_specs=out_specs, check_vma=False)
```

time: 829 us -> 133 us (0.16); the launches traced: 815 us -> 132 us
  local copies, waits for them, and re-layouts: 400 us -> 2.87 us
  matrix products: 205 us -> 0 us
  other arithmetic: 145 us -> 4.15 us
  waiting for transfers between devices: 26.8 us -> 68.3 us
  Pallas kernels: 0 us -> 33.3 us
  blocking collectives: 21 us -> 9.45 us
    dynamic_update_slice x72 -> x0, local copies, waits for them, and re-layouts: 283 us -> none  [slab_core(): lax.scan(span_step, start, (stacked, decay_blocks, b_blocks, c_blocks))]
    dot_general x99 -> x0, matrix products: 205 us -> none  [the longest x24 59.4 us: span_step(): jnp.einsum('hij,jhp->ihp', mixing, values.astype(jnp.bfloat16), preferred...]
    dynamic_update_slice x48 -> x0, other arithmetic: 72 us -> none  [slab_core(): lax.scan(span_step, start, (stacked, decay_blocks, b_blocks, c_blocks))]
    unnamed x53 -> x1, local copies, waits for them, and re-layouts: 43.5 us -> 0.11 us
    another operation x64 -> x0, other arithmetic: 42.3 us -> none
    pallas_call x0 -> x2, Pallas kernels: none -> 33.3 us  [the longest x1 22.7 us: shards(): pl.pallas_call(functools.partial(core_kernel, heads, width), grid=(blocks...]
    dynamic_slice x40 -> x0, local copies, waits for them, and re-layouts: 32.2 us -> none  [slab_core(): lax.scan(span_step, start, (stacked, decay_blocks, b_blocks, c_blocks))]
    reduce_scatter x2 -> x1, waiting for transfers between devices: 2.7 us -> 25.6 us  [shards(): shared = lax.psum_scatter(gbc, 'head', scatter_dimension=0, tiled=True)]
  transfers between devices with their start and end apart: 4 -> 2, of which waited for: 2 -> 2; matrix products, arithmetic and copies ran while one was open for 9% -> 1% of each run, Pallas kernels for 0% -> 0%
where the time goes in v1:
time: 133 us; the launch traced here: 132 us
  waiting for transfers between devices  68.3 us (51%)
  Pallas kernels  33.3 us (25%)
  between operations  14.1 us (11%)
  blocking collectives  9.45 us (7%)
  other arithmetic  4.15 us (3%)
  local copies, waits for them, and re-layouts  2.87 us (2%)
    all_gather x1, waiting for transfers between devices, shards(): pieces = lax.all_gather(packed, 'seq')  42.7 us
    reduce_scatter x1, waiting for transfers between devices, shards(): shared = lax.psum_scatter(gbc, 'head', scatter_dimension=0, tiled=True)  25.6 us
    pallas_call x1, Pallas kernels, shards(): pl.pallas_call(functools.partial(core_kernel, heads, width), grid=(blocks...  22.7 us
    pallas_call x1, Pallas kernels, shards(): pl.pallas_call(functools.partial(states_kernel, heads, width), grid=(bloc...  10.5 us
    psum x1, blocking collectives, shards(): head_grads = lax.psum(jnp.sum(sums_out, axis=2), 'seq')  9.45 us
    reduce_sum x1, other arithmetic, shards(): jnp.sum(weight_out[:, :, None, None] * adjoints, axis=0).reshape(size, n)  3.05 us
  transfers between devices with their start and end apart: 2, of which 2 were waited for; matrix products, arithmetic and copies ran while one was open for 1% of the time, Pallas kernels for 0%

profile of v1, /device:TPU:0, one launch (start us, length us, event | category | flops | bytes accessed | tf_op | source)
XLA Modules:
  0.0 132.2 jit_solution(10504784203047629204)
XLA Ops:
  7.2 0.0 all-gather.3.cloned.1.call-start
  7.2 10.5 %shard_map.100 = (bf16[640,2048]{1,0:T(8,128)(2,1)}, bf16[640,2048]{1,0:T(8,128)(2,1)}, f32[10,2048]{1,0:T(8,128)}, f32[8,640,128]{2,1,0:T(8,128)}, f32[8,10,128]{2,1,0:T(8,128)}, /*index=5*/f32[1296,128]{1,0:T(8,128)}) custom-call(bf16[2048,640]{1,0:T(8,128)(2,1)} %x_ref.1, bf16[2048,640]{1,0:T(8,128)(2,1)} %dy_ref.1, f32[10,2048]{1,0:T(8,128)} %a_ref.3, ...), custom_call_target="tpu_custom_call" | custom-call | tf_op jit(solution)/shard_map/pallas_call | solution.py:159
  17.7 0.0 all-gather.3.cloned.1.call-update
  17.8 0.0 reduce-scatter.2.cloned.1.call-start
  17.9 42.7 %all-gather.3.cloned.1.call-done = f32[5184,128]{1,0:T(8,128)} async-done(((f32[1296,128]{1,0:T(8,128)}), f32[5184,128]{1,0:T(8,128)}) %all-gather.3.cloned.1.call-update) | async-done | bytes 2654224 | tf_op jit(solution)/shard_map/all_gather | solution.py:175
  60.5 0.8 slice.20
  61.3 0.1 copy.14
  61.4 0.1 select_reduce_fusion
  61.5 0.1 exponential_select_fusion
  61.6 0.1 exponential_select_fusion.1
  61.6 0.1 mul.26
  61.7 0.1 mul.27
  61.8 0.1 mul.30
  61.9 0.1 mul.31
  62.0 3.1 %fusion = (f32[640,128]{1,0:T(8,128)}, f32[640,128]{1,0:T(8,128)}) fusion(f32[4,1296,128]{2,1,0:T(8,128)} %bitcast.3, f32[4,640]{1,0:T(4,128)S(1)} %mul.31, f32[4,640]{1,0:T(4,128)S(1)} %mul.27), kind=kLoop, calls=%fused_computation.1 | loop fusion | flops 1146880 | bytes 3297280 | tf_op jit(solution)/shard_map/reduce_sum | solution.py:188
  65.0 22.7 %shard_map.101 = (f32[2048,640]{1,0:T(8,128)}, f32[2048,640]{1,0:T(8,128)}, f32[10,2048]{1,0:T(8,128)}, f32[2048,256]{1,0:T(8,128)}, f32[2,10,256]{2,1,0:T(8,128)}) custom-call(bf16[640,2048]{1,0:T(8,128)(2,1)} %get-tuple-element.17.xt_ref, bf16[640,2048]{1,0:T(8,128)(2,1)} %get-tuple-element.18.dyt_ref, f32[10,2048]{1,0:T(8,128)} %a_ref.3, ...), custom_call_target="tpu_custom_call" | custom-call | tf_op jit(solution)/shard_map/pallas_call | solution.py:196
  87.7 0.0 reduce-scatter.2.cloned.1.call-update
  87.8 0.8 reduce_sum.49
  88.6 9.4 %psum.7 = f32[2,10]{1,0:T(2,128)} all-reduce(f32[2,10]{1,0:T(2,128)S(1)} %reduce_sum.49), channel_id=1, replica_groups=mesh['seq'=4,'head'=8] {'seq'}, use_global_device_ids=true, to_apply=%region_6.7 | all-reduce | flops 20 | bytes 160 | tf_op jit(solution)/shard_map/psum | solution.py:217
  98.1 25.6 %reduce-scatter.2.cloned.1.call-done = f32[256,256]{1,0:T(8,128)} async-done(((f32[2048,256]{1,0:T(8,128)}), f32[256,256]{1,0:T(8,128)}) %reduce-scatter.2.cloned.1.call-update) | async-done | bytes 262160 | tf_op jit(solution)/shard_map/reduce_scatter | solution.py:216
  123.7 1.7 %fusion.4 = (f32[256,128]{1,0:T(8,128)}, f32[256,128]{1,0:T(8,128)}) fusion(f32[256,256]{1,0:T(8,128)} %reduce-scatter.2.cloned.1.call-done), kind=kLoop, calls=%fused_computation.14 | loop fusion | bytes 524288 | tf_op jit(solution)/shard_map/slice | solution.py:218
  (3 shorter events, 0.0 us)
Async XLA Ops:
  7.2 53.4 %all-gather.3.cloned.1.call-start = ((), (), s32[]{:S(2)}) async-start(), calls=%async_computation.2 | async-start | bytes 3317760 | tf_op jit(solution)/shard_map/all_gather | solution.py:175
  17.8 105.9 %reduce-scatter.2.cloned.1.call-start = ((), (), s32[]{:S(2)}) async-start(), calls=%async_computation.1 | async-start | bytes 2359296 | tf_op jit(solution)/shard_map/reduce_scatter | solution.py:216
Sparse Core Ops, SparseCore 0:
  17.9 42.6 all-gather.2
  87.9 35.7 reduce-scatter.1

commit v2 on v1

v2 whole, which is shorter than its diff:
```python
import functools

import jax
import jax.numpy as jnp
from jax import lax
from jax.experimental import pallas as pl
from jax.experimental.pallas import tpu as pltpu
from jax.sharding import PartitionSpec as P

SPAN = 256
F32 = jnp.float32
BF16 = jnp.bfloat16
NN = (((1,), (0,)), ((), ()))
NT = (((1,), (1,)), ((), ()))
TN = (((0,), (0,)), ((), ()))


def mm(left, right, dims):
    return lax.dot_general(left, right, dims, preferred_element_type=F32)


def sums(left, right):
    return jnp.dot(left, right, precision=lax.Precision.HIGHEST, preferred_element_type=F32)


def indices():
    rows = lax.broadcasted_iota(jnp.int32, (SPAN, SPAN), 0)
    columns = lax.broadcasted_iota(jnp.int32, (SPAN, SPAN), 1)
    return rows, columns


def states_kernel(heads, width, x_ref, dy_ref, a_ref, b_ref, c_ref,
                  xt_ref, dyt_ref, cum_ref, entry_ref, before_ref, packed_ref, sum_ref):
    k = pl.program_id(0)
    size = heads * width

    @pl.when(k == 0)
    def _():
        packed_ref[...] = jnp.zeros_like(packed_ref)
        sum_ref[...] = jnp.zeros_like(sum_ref)

    x_t = x_ref[...].astype(F32).T
    dy_t = dy_ref[...].astype(F32).T
    xt_ref[...] = x_t.astype(BF16)
    dyt_ref[...] = dy_t.astype(BF16)
    rows, columns = indices()
    cum = sums(a_ref[...], (rows <= columns).astype(F32))
    cum_ref[...] = cum
    last = cum[:, SPAN - 1:]
    head_decay = jnp.exp(cum)
    tail = jnp.exp(last - cum)
    scaled, weighted = [], []
    for h in range(heads):
        part = slice(h * width, (h + 1) * width)
        scaled.append((x_t[part] * tail[h:h + 1]).astype(BF16))
        weighted.append((dy_t[part] * head_decay[h:h + 1]).astype(BF16))
    update = mm(jnp.concatenate(scaled, axis=0), b_ref[...], NN)
    own = mm(jnp.concatenate(weighted, axis=0), c_ref[...], NN)
    before = sum_ref[...]
    before_ref[0] = jnp.exp(before)
    entry_ref[0] = packed_ref[:size]
    for h in range(heads):
        part = slice(h * width, (h + 1) * width)
        later = slice(size + h * width, size + (h + 1) * width)
        packed_ref[part] = packed_ref[part] * jnp.exp(last[h:h + 1]) + update[part]
        packed_ref[later] = packed_ref[later] + jnp.exp(before[h:h + 1]) * own[part]
    sum_ref[...] = before + last
    packed_ref[2 * size:2 * size + heads] = before + last


def local_kernel(heads, width, xt_ref, dyt_ref, cum_ref, b_ref, c_ref,
                 inner_ref, back_ref, gain_ref, gbc_ref, skip_ref, gs_ref):
    state_size = b_ref.shape[1]

    @pl.when(pl.program_id(0) == 0)
    def _():
        skip_ref[...] = jnp.zeros_like(skip_ref)

    rows, columns = indices()
    lower = rows <= columns
    cum = cum_ref[...]
    cum_columns = jnp.concatenate(
        [cum, jnp.zeros((-heads % 8, SPAN), F32)] if heads % 8 else [cum], axis=0).T
    b, c = b_ref[...], c_ref[...]
    scores = mm(b, c, NT)
    gain, skip = [], []
    for h in range(heads):
        part = slice(h * width, (h + 1) * width)
        weights = jnp.where(lower, jnp.exp(cum[h:h + 1] - cum_columns[:, h:h + 1]), 0.0)
        mixing = (weights * scores).astype(BF16)
        x_half, dy_half = xt_ref[part], dyt_ref[part]
        inner = mm(x_half, mixing, NN)
        back = mm(dy_half, mixing, NT)
        piece = weights * mm(x_half, dy_half, TN)
        if h == 0:
            gs_ref[...] = piece
        else:
            gs_ref[...] += piece
        x, dy = x_half.astype(F32), dy_half.astype(F32)
        inner_ref[part] = inner
        back_ref[part] = back
        gain.append(jnp.sum(dy * inner - x * back, axis=0, keepdims=True))
        skip.append(jnp.sum(x * dy, axis=0, keepdims=True))
    gain_ref[...] = jnp.concatenate(gain, axis=0)
    skip_ref[...] += jnp.concatenate(skip, axis=0)
    gs_half = gs_ref[...].astype(BF16)
    gbc_ref[:, :state_size] = mm(gs_half, c, NN)
    gbc_ref[:, state_size:] = mm(gs_half, b, TN)


def maps_kernel(heads, width, xt_ref, dyt_ref, cum_ref, c_ref, local_ref, before_ref,
                entry_ref, after_ref, part_ref, gbc_ref, state_ref, adjoint_ref, edge_ref,
                adj_ref, st_ref, scaled_ref, weighted_ref):
    state_size = c_ref.shape[1]

    @pl.when(pl.program_id(0) == 0)
    def _():
        adj_ref[...] = after_ref[...]

    cum = cum_ref[...]
    last = cum[:, SPAN - 1:]
    head_decay = jnp.exp(cum)
    tail = jnp.exp(last - cum)
    whole = jnp.exp(last)
    before = before_ref[0]
    edge = []
    for h in range(heads):
        part = slice(h * width, (h + 1) * width)
        state = local_ref[0, part] + before[h:h + 1] * entry_ref[part]
        st_ref[part] = state.astype(BF16)
        products = jnp.sum(state * adj_ref[part], axis=0, keepdims=True)
        edge.append(jnp.sum(products, axis=1, keepdims=True) * whole[h:h + 1])
        scaled_ref[part] = (xt_ref[part].astype(F32) * tail[h:h + 1]).astype(BF16)
        weighted_ref[part] = (dyt_ref[part].astype(F32) * head_decay[h:h + 1]).astype(BF16)
    state_half = st_ref[...]
    adj_half = adj_ref[...].astype(BF16)
    state_ref[0] = state_half
    adjoint_ref[0] = adj_half
    edge_ref[0] = jnp.broadcast_to(jnp.concatenate(edge, axis=0), edge_ref.shape[1:])
    gbc_ref[:, :state_size] = part_ref[:, :state_size] + mm(scaled_ref[...], adj_half, TN)
    gbc_ref[:, state_size:] = part_ref[:, state_size:] + mm(weighted_ref[...], state_half, TN)
    own = mm(weighted_ref[...], c_ref[...], NN)
    for h in range(heads):
        part = slice(h * width, (h + 1) * width)
        adj_ref[part] = adj_ref[part] * whole[h:h + 1] + own[part]


def output_kernel(heads, width, xt_ref, dyt_ref, a_ref, cum_ref, b_ref, c_ref, inner_ref, back_ref,
                  gain_ref, state_ref, adjoint_ref, edge_ref,
                  y_ref, gx_ref, ga_ref, rate_ref, yt_ref, gxt_ref):
    @pl.when(pl.program_id(0) == 0)
    def _():
        rate_ref[...] = jnp.zeros_like(rate_ref)

    rows, columns = indices()
    cum = cum_ref[...]
    last = cum[:, SPAN - 1:]
    head_decay = jnp.exp(cum)
    tail = jnp.exp(last - cum)
    carried_all = mm(state_ref[0], c_ref[...], NT)
    scaled_grad_all = mm(adjoint_ref[0], b_ref[...], NT)
    gain, loss = [], []
    for h in range(heads):
        part = slice(h * width, (h + 1) * width)
        x, dy = xt_ref[part].astype(F32), dyt_ref[part].astype(F32)
        carried = carried_all[part] * head_decay[h:h + 1]
        tailed = scaled_grad_all[part] * tail[h:h + 1]
        yt_ref[part] = inner_ref[part] + carried + x
        gxt_ref[part] = back_ref[part] + tailed + dy
        gain.append(jnp.sum(dy * carried, axis=0, keepdims=True))
        loss.append(jnp.sum(x * tailed, axis=0, keepdims=True))
    y_ref[...] = yt_ref[...].T
    gx_ref[...] = gxt_ref[...].T
    grad = (sums(gain_ref[...] + jnp.concatenate(gain, axis=0), (rows >= columns).astype(F32))
            + sums(jnp.concatenate(loss, axis=0), (rows < columns).astype(F32))
            + edge_ref[0][:, :1])
    ga_ref[...] = grad
    rate_ref[...] += grad * a_ref[...]


def gathered(packed, heads, width, n):
    size = heads * width
    count, mine = lax.axis_size("seq"), lax.axis_index("seq")
    pieces = lax.all_gather(packed, "seq")
    totals = pieces[:, 2 * size:2 * size + heads, 0]
    states = pieces[:, :size].reshape(count, heads, width, n)
    adjoints = pieces[:, size:2 * size].reshape(count, heads, width, n)
    place = jnp.arange(count)
    mid = place[None, :]
    ahead = (mid > place[:, None]) & (mid < mine)
    behind = (mid < place[:, None]) & (mid > mine)
    gap_in = jnp.sum(jnp.where(ahead[:, :, None], totals[None], 0.0), axis=1)
    gap_out = jnp.sum(jnp.where(behind[:, :, None], totals[None], 0.0), axis=1)
    weight_in = jnp.where((place < mine)[:, None], jnp.exp(gap_in), 0.0)
    weight_out = jnp.where((place > mine)[:, None], jnp.exp(gap_out), 0.0)
    entry = jnp.sum(weight_in[:, :, None, None] * states, axis=0).reshape(size, n)
    after = jnp.sum(weight_out[:, :, None, None] * adjoints, axis=0).reshape(size, n)
    return entry, after


def exchanged(packed, heads, width, n):
    size = heads * width
    mine = lax.axis_index("seq")
    state = jnp.concatenate([packed[:size], packed[2 * size:]], axis=0)
    adjoint = packed[size:]
    by_x = lax.ppermute(jnp.where(mine % 2 == 0, state, adjoint), "seq",
                        [(0, 1), (1, 0), (2, 3), (3, 2)])
    by_y = lax.ppermute(jnp.where(mine < 2, state, adjoint), "seq",
                        [(0, 2), (2, 0), (1, 3), (3, 1)])
    far = (lax.ppermute(by_y, "seq", [(0, 1), (3, 2)])
           + lax.ppermute(by_x, "seq", [(1, 3), (2, 0)]))

    def cut(value):
        return value[:size].reshape(heads, width, n), value[size:size + heads, :1, None]

    (near, near_sum), (side, side_sum), (last, last_sum) = cut(by_x), cut(by_y), cut(far)
    whole = near + jnp.exp(near_sum) * side + jnp.exp(near_sum + side_sum) * last
    double = last + jnp.exp(last_sum) * side
    zero = jnp.zeros_like(near)
    entry = jnp.where(mine == 0, zero, jnp.where(mine == 1, near, jnp.where(mine == 2, double, whole)))
    after = jnp.where(mine == 3, zero, jnp.where(mine == 2, near, jnp.where(mine == 1, double, whole)))
    return entry.reshape(size, n), after.reshape(size, n)


def shards(signal, log_decay, b_matrix, c_matrix, out_grad):
    length, size = signal.shape
    heads = log_decay.shape[0]
    width = size // heads
    n = b_matrix.shape[1]
    blocks = length // SPAN
    padded = -(-(2 * size + heads) // 8) * 8
    shape = jax.ShapeDtypeStruct
    params = pltpu.CompilerParams(vmem_limit_bytes=56 * 2**20)

    token = pl.BlockSpec((SPAN, size), lambda k: (k, 0))
    flat = pl.BlockSpec((size, SPAN), lambda k: (0, k))
    decay = pl.BlockSpec((heads, SPAN), lambda k: (0, k))
    maps = pl.BlockSpec((SPAN, n), lambda k: (k, 0))
    xt, dyt, cum, local, before, packed = pl.pallas_call(
        functools.partial(states_kernel, heads, width),
        grid=(blocks,),
        in_specs=[token, token, decay, maps, maps],
        out_specs=[flat, flat, decay,
                   pl.BlockSpec((1, size, n), lambda k: (k, 0, 0)),
                   pl.BlockSpec((1, heads, n), lambda k: (k, 0, 0)),
                   pl.BlockSpec((padded, n), lambda k: (0, 0))],
        out_shape=[shape((size, length), BF16), shape((size, length), BF16),
                   shape((heads, length), F32), shape((blocks, size, n), F32),
                   shape((blocks, heads, n), F32), shape((padded, n), F32)],
        scratch_shapes=[pltpu.VMEM((heads, n), F32)],
        compiler_params=params,
    )(signal, out_grad, log_decay, b_matrix, c_matrix)

    def grad_cost(micros):
        return pl.CostEstimate(flops=int(micros * 1.0e9), bytes_accessed=int(micros * 3.0e6),
                               transcendentals=0)

    per_block = pl.BlockSpec((1, heads, n), lambda k: (k, 0, 0))
    pair = pl.BlockSpec((SPAN, 2 * n), lambda k: (k, 0))
    once = pl.BlockSpec((heads, SPAN), lambda k: (0, 0))
    inner, back, gain, local_maps, skip = pl.pallas_call(
        functools.partial(local_kernel, heads, width),
        grid=(blocks,),
        in_specs=[flat, flat, decay, maps, maps],
        out_specs=[flat, flat, decay, pair, once],
        out_shape=[shape((size, length), F32), shape((size, length), F32),
                   shape((heads, length), F32), shape((length, 2 * n), F32),
                   shape((heads, SPAN), F32)],
        scratch_shapes=[pltpu.VMEM((SPAN, SPAN), F32)],
        compiler_params=params, cost_estimate=grad_cost(18),
    )(xt, dyt, cum, b_matrix, c_matrix)

    exchange = exchanged if lax.axis_size("seq") == 4 else gathered
    entry, after = exchange(packed, heads, width, n)

    end = blocks - 1
    r_flat = pl.BlockSpec((size, SPAN), lambda k: (0, end - k))
    r_state = pl.BlockSpec((1, size, n), lambda k: (end - k, 0, 0))
    r_block = pl.BlockSpec((1, heads, n), lambda k: (end - k, 0, 0))
    r_pair = pl.BlockSpec((SPAN, 2 * n), lambda k: (end - k, 0))
    edge_spec = pl.BlockSpec((size, n), lambda k: (0, 0))
    gbc, state_half, adj_half, edge = pl.pallas_call(
        functools.partial(maps_kernel, heads, width),
        grid=(blocks,),
        in_specs=[r_flat, r_flat, pl.BlockSpec((heads, SPAN), lambda k: (0, end - k)),
                  pl.BlockSpec((SPAN, n), lambda k: (end - k, 0)), r_state, r_block,
                  edge_spec, edge_spec, r_pair],
        out_specs=[r_pair, r_state, r_state, r_block],
        out_shape=[shape((length, 2 * n), F32), shape((blocks, size, n), BF16),
                   shape((blocks, size, n), BF16), shape((blocks, heads, n), F32)],
        scratch_shapes=[pltpu.VMEM((size, n), F32), pltpu.VMEM((size, n), BF16),
                        pltpu.VMEM((size, SPAN), BF16), pltpu.VMEM((size, SPAN), BF16)],
        compiler_params=params, cost_estimate=grad_cost(6),
    )(xt, dyt, cum, c_matrix, local, before, entry, after, local_maps)

    shared = lax.psum_scatter(gbc, "head", scatter_dimension=0, tiled=True)

    state_spec = pl.BlockSpec((1, size, n), lambda k: (k, 0, 0))
    y, gx, ga, rate = pl.pallas_call(
        functools.partial(output_kernel, heads, width),
        grid=(blocks,),
        in_specs=[flat, flat, decay, decay, maps, maps, flat, flat, decay,
                  state_spec, state_spec, per_block],
        out_specs=[token, token, decay, once],
        out_shape=[shape((length, size), F32), shape((length, size), F32),
                   shape((heads, length), F32), shape((heads, SPAN), F32)],
        scratch_shapes=[pltpu.VMEM((size, SPAN), F32), pltpu.VMEM((size, SPAN), F32)],
        compiler_params=params, cost_estimate=grad_cost(14),
    )(xt, dyt, log_decay, cum, b_matrix, c_matrix, inner, back, gain, state_half, adj_half, edge)

    head_grads = lax.psum(jnp.stack([jnp.sum(skip, axis=1), jnp.sum(rate, axis=1)]), "seq")
    return y, gx, ga, shared[:, :n], shared[:, n:], head_grads


def solution(mesh):
    in_specs = (
        P("seq", "head"),
        P("head", "seq"),
        P("seq", None),
        P("seq", None),
        P("seq", "head"),
    )
    out_specs = (
        P("seq", "head"),
        P("seq", "head"),
        P("head", "seq"),
        P(("seq", "head"), None),
        P(("seq", "head"), None),
        P(None, "head"),
    )
    return jax.shard_map(shards, mesh=mesh, in_specs=in_specs, out_specs=out_specs, check_vma=False)
```

time: 133 us -> 110 us (0.83)
  waiting for transfers between devices: 68.3 us -> 17.7 us
  Pallas kernels: 33.3 us -> 48.9 us
  starting transfers between devices: 0.08 us -> 9.48 us
    all_gather x1 -> x0, waiting for transfers between devices: 42.7 us -> none  [shards(): pieces = lax.all_gather(packed, 'seq')]
    pallas_call x1 -> x3, Pallas kernels: 22.7 us -> 38.3 us  [the longest x1 14.4 us: shards(): pl.pallas_call(functools.partial(output_kernel, heads, width), grid=(bloc...]
    reduce_scatter x1, waiting for transfers between devices: 25.6 us -> 11.3 us  [shards(): shared = lax.psum_scatter(gbc, 'head', scatter_dimension=0, tiled=True)]
    ppermute x0 -> x4, starting transfers between devices: none -> 9.44 us  [the longest x1 3.62 us: exchanged(): lax.ppermute(by_y, 'seq', [(0, 1), (3, 2)])]
    ppermute x0 -> x4, waiting for transfers between devices: none -> 6.4 us  [the longest x1 6.39 us: exchanged(): lax.ppermute(jnp.where(mine < 2, state, adjoint), 'seq', [(0, 2), (2, 0),...]
    reduce_sum x3 -> x2, other arithmetic: 3.99 us -> 0.95 us  [the longest x1 0.84 us: shards(): jnp.sum(rate, axis=1)]
    select_n x2 -> x3, other arithmetic: 0.13 us -> 2.98 us  [the longest x1 1.06 us: exchanged(): jnp.where(mine == 3, zero, jnp.where(mine == 2, near, jnp.where(mine == 1...]
  transfers between devices with their start and end apart: 2 -> 5, of which waited for: 2 -> 2; matrix products, arithmetic and copies ran while one was open for 1% -> 1% of each run, Pallas kernels for 0% -> 26%
where the time goes in v2:
time: 110 us; the launch traced here: 109 us
  Pallas kernels  48.9 us (44%)
  waiting for transfers between devices  17.7 us (16%)
  between operations  14.1 us (13%)
  blocking collectives  10.7 us (10%)
  starting transfers between devices  9.48 us (9%)
  other arithmetic  4.11 us (4%)
  local copies, waits for them, and re-layouts  3.93 us (4%)
    pallas_call x1, Pallas kernels, shards(): pl.pallas_call(functools.partial(output_kernel, heads, width), grid=(bloc...  14.4 us
    pallas_call x1, Pallas kernels, shards(): pl.pallas_call(functools.partial(local_kernel, heads, width), grid=(block...  13.9 us
    reduce_scatter x1, waiting for transfers between devices, shards(): shared = lax.psum_scatter(gbc, 'head', scatter_dimension=0, tiled=True)  11.3 us
    psum x1, blocking collectives, shards(): lax.psum(jnp.stack([jnp.sum(skip, axis=1), jnp.sum(rate, axis=1)]), 'seq')  10.7 us
    pallas_call x1, Pallas kernels, shards(): pl.pallas_call(functools.partial(states_kernel, heads, width), grid=(bloc...  10.5 us
    pallas_call x1, Pallas kernels, shards(): pl.pallas_call(functools.partial(maps_kernel, heads, width), grid=(blocks...  10.1 us
    ppermute x1, waiting for transfers between devices, exchanged(): lax.ppermute(jnp.where(mine < 2, state, adjoint), 'seq', [(0, 2), (2, 0),...  6.39 us
    ppermute x1, starting transfers between devices, exchanged(): lax.ppermute(by_y, 'seq', [(0, 1), (3, 2)])  3.62 us
  transfers between devices with their start and end apart: 5, of which 2 were waited for; matrix products, arithmetic and copies ran while one was open for 1% of the time, Pallas kernels for 26%

profile of v2, /device:TPU:0, one launch (start us, length us, event | category | flops | bytes accessed | tf_op | source)
XLA Modules:
  0.0 108.9 jit_solution(17757176875781533778)
XLA Ops:
  7.2 0.0 reduce-scatter.2.cloned.1.call-start
  7.2 10.5 %shard_map.100 = (bf16[640,2048]{1,0:T(8,128)(2,1)}, bf16[640,2048]{1,0:T(8,128)(2,1)}, f32[10,2048]{1,0:T(8,128)}, f32[8,640,128]{2,1,0:T(8,128)}, f32[8,10,128]{2,1,0:T(8,128)}, /*index=5*/f32[1296,128]{1,0:T(8,128)}) custom-call(bf16[2048,640]{1,0:T(8,128)(2,1)} %x_ref.1, bf16[2048,640]{1,0:T(8,128)(2,1)} %dy_ref.1, f32[10,2048]{1,0:T(8,128)} %a_ref.3, ...), custom_call_target="tpu_custom_call" | custom-call | tf_op jit(solution)/shard_map/pallas_call | solution.py:239
  17.8 0.7 slice.34
  18.5 1.0 slice.33
  19.5 1.0 slice_select_fusion
  20.5 3.0 %collective-permute-start.1 = (f32[656,128]{1,0:T(8,128)S(1)}, f32[656,128]{1,0:T(8,128)S(1)}, u32[]{:S(2)}, u32[]{:S(2)}) collective-permute-start(f32[656,128]{1,0:T(8,128)S(1)} %get-tuple-element.48), channel_id=1, source_target_pairs={{0,16},{16,0},{8,24},{24,8},{1,17},{17,1},{9,25},{25,9},{2,18},{18... | collective-permute-start | bytes 1007624 | tf_op jit(solution)/shard_map/ppermute | solution.py:208
  23.5 1.5 %collective-permute-start = (f32[656,128]{1,0:T(8,128)S(1)}, f32[656,128]{1,0:T(8,128)S(1)}, u32[]{:S(2)}, u32[]{:S(2)}) collective-permute-start(f32[656,128]{1,0:T(8,128)S(1)} %get-tuple-element.49), channel_id=1, source_target_pairs={{0,8},{8,0},{16,24},{24,16},{1,9},{9,1},{17,25},{25,17},{2,10},{10... | collective-permute-start | bytes 1007624 | tf_op jit(solution)/shard_map/ppermute | solution.py:206
  25.0 6.4 %collective-permute-done.1 = f32[656,128]{1,0:T(8,128)S(1)} collective-permute-done((f32[656,128]{1,0:T(8,128)S(1)}, f32[656,128]{1,0:T(8,128)S(1)}, u32[]{:S(2)}, u32[]{:S(2)}) %collective-permute-start.1) | collective-permute-done | bytes 335904 | tf_op jit(solution)/shard_map/ppermute | solution.py:208
  31.4 3.6 %collective-permute-start.2 = (f32[656,128]{1,0:T(8,128)S(1)}, f32[656,128]{1,0:T(8,128)S(1)}, u32[]{:S(2)}, u32[]{:S(2)}) collective-permute-start(f32[656,128]{1,0:T(8,128)S(1)} %collective-permute-done.1), channel_id=1, source_target_pairs={{0,8},{24,16},{1,9},{25,17},{2,10},{26,18},{3,11},{27,19},{4,12},{... | collective-permute-start | bytes 1007624 | tf_op jit(solution)/shard_map/ppermute | solution.py:210
  35.0 0.0 collective-permute-done
  35.0 1.3 %collective-permute-start.3 = (f32[656,128]{1,0:T(8,128)S(1)}, f32[656,128]{1,0:T(8,128)S(1)}, u32[]{:S(2)}, u32[]{:S(2)}) collective-permute-start(f32[656,128]{1,0:T(8,128)S(1)} %collective-permute-done), channel_id=1, source_target_pairs={{8,24},{16,0},{9,25},{17,1},{10,26},{18,2},{11,27},{19,3},{12,28},... | collective-permute-start | bytes 1007624 | tf_op jit(solution)/shard_map/ppermute | solution.py:211
  36.4 13.9 %shard_map.101 = (f32[640,2048]{1,0:T(8,128)}, f32[640,2048]{1,0:T(8,128)}, f32[10,2048]{1,0:T(8,128)}, f32[2048,256]{1,0:T(8,128)}, f32[10,256]{1,0:T(8,128)}) custom-call(bf16[640,2048]{1,0:T(8,128)(2,1)} %get-tuple-element.25.xt_ref, bf16[640,2048]{1,0:T(8,128)(2,1)} %get-tuple-element.26.dyt_ref, f32[10,2048]{1,0:T(8,128)} %get-tuple-element.27.cum_ref, ...), custom_call_target="tpu_custom_call" | custom-call | flops 17999998976 | bytes 54000000 | tf_op jit(solution)/shard_map/pallas_call | solution.py:261
  50.2 0.1 exponential_reduce_fusion
  50.3 0.1 mul.46
  50.4 0.1 mul.47
  50.5 0.1 mul.50
  50.6 0.1 mul.51
  50.6 0.0 collective-permute-done.2
  50.6 0.0 collective-permute-done.3
  50.7 0.1 fusion.2
  50.8 0.1 mul.42
  50.9 0.1 mul.43
  51.0 1.1 select_select_fusion
  52.0 0.9 select_select_fusion.1.entry_ref
  52.9 0.0 copy-start
  52.9 10.1 %shard_map.102 = (f32[2048,256]{1,0:T(8,128)}, bf16[8,640,128]{2,1,0:T(8,128)(2,1)}, bf16[8,640,128]{2,1,0:T(8,128)(2,1)}, f32[8,10,128]{2,1,0:T(8,128)}) custom-call(bf16[640,2048]{1,0:T(8,128)(2,1)} %get-tuple-element.25.xt_ref, bf16[640,2048]{1,0:T(8,128)(2,1)} %get-tuple-element.26.dyt_ref, f32[10,2048]{1,0:T(8,128)} %get-tuple-element.27.cum_ref, ...), custom_call_target="tpu_custom_call" | custom-call | flops 6000000000 | bytes 18000000 | tf_op jit(solution)/shard_map/pallas_call | solution.py:282
  63.0 0.0 reduce-scatter.2.cloned.1.call-update
  63.0 0.0 copy-done
  63.0 0.1 reduce_sum.18
  63.1 14.4 %shard_map.103 = (f32[2048,640]{1,0:T(8,128)}, f32[2048,640]{1,0:T(8,128)}, f32[10,2048]{1,0:T(8,128)}, f32[10,256]{1,0:T(8,128)}) custom-call(bf16[640,2048]{1,0:T(8,128)(2,1)} %get-tuple-element.25.xt_ref, bf16[640,2048]{1,0:T(8,128)(2,1)} %get-tuple-element.26.dyt_ref, f32[10,2048]{1,0:T(8,128)} %a_ref.3, f32[10,2048]{1,0:T(8,128)} %get-tuple-element.27.cum_ref, ...), custom_call_target="tpu_custom_call" | custom-call | flops 14000000000 | bytes 42000000 | tf_op jit(solution)/shard_map/pallas_call | solution.py:299
  77.5 0.8 reduce_sum.19
  78.4 10.7 %psum.7 = f32[2,10]{1,0:T(2,128)} all-reduce(f32[2,10]{1,0:T(2,128)S(1)} %pad_maximum_fusion.1), channel_id=1, replica_groups=mesh['seq'=4,'head'=8] {'seq'}, use_global_device_ids=true, to_apply=%region_3.4 | all-reduce | flops 20 | bytes 160 | tf_op jit(solution)/shard_map/psum | solution.py:311
  89.1 11.3 %reduce-scatter.2.cloned.1.call-done = f32[256,256]{1,0:T(8,128)} async-done(((f32[2048,256]{1,0:T(8,128)}), f32[256,256]{1,0:T(8,128)}) %reduce-scatter.2.cloned.1.call-update) | async-done | bytes 262160 | tf_op jit(solution)/shard_map/reduce_scatter | solution.py:296
  100.4 1.7 %fusion.3 = (f32[256,128]{1,0:T(8,128)}, f32[256,128]{1,0:T(8,128)}) fusion(f32[256,256]{1,0:T(8,128)} %reduce-scatter.2.cloned.1.call-done), kind=kLoop, calls=%fused_computation.14 | loop fusion | bytes 524288 | tf_op jit(solution)/shard_map/slice | solution.py:312
  (2 shorter events, 0.1 us)
Async XLA Ops:
  7.2 93.2 %reduce-scatter.2.cloned.1.call-start = ((), (), s32[]{:S(2)}) async-start(), calls=%async_computation.1 | async-start | bytes 2359296 | tf_op jit(solution)/shard_map/reduce_scatter | solution.py:296
  20.5 10.9 %collective-permute-start.1 = (f32[656,128]{1,0:T(8,128)S(1)}, f32[656,128]{1,0:T(8,128)S(1)}, u32[]{:S(2)}, u32[]{:S(2)}) collective-permute-start(f32[656,128]{1,0:T(8,128)S(1)} %get-tuple-element.48), channel_id=1, source_target_pairs={{0,16},{16,0},{8,24},{24,8},{1,17},{17,1},{9,25},{25,9},{2,18},{18... | collective-permute-start | bytes 1007624 | tf_op jit(solution)/shard_map/ppermute | solution.py:208
  23.5 11.5 %collective-permute-start = (f32[656,128]{1,0:T(8,128)S(1)}, f32[656,128]{1,0:T(8,128)S(1)}, u32[]{:S(2)}, u32[]{:S(2)}) collective-permute-start(f32[656,128]{1,0:T(8,128)S(1)} %get-tuple-element.49), channel_id=1, source_target_pairs={{0,8},{8,0},{16,24},{24,16},{1,9},{9,1},{17,25},{25,17},{2,10},{10... | collective-permute-start | bytes 1007624 | tf_op jit(solution)/shard_map/ppermute | solution.py:206
  31.4 19.2 %collective-permute-start.2 = (f32[656,128]{1,0:T(8,128)S(1)}, f32[656,128]{1,0:T(8,128)S(1)}, u32[]{:S(2)}, u32[]{:S(2)}) collective-permute-start(f32[656,128]{1,0:T(8,128)S(1)} %collective-permute-done.1), channel_id=1, source_target_pairs={{0,8},{24,16},{1,9},{25,17},{2,10},{26,18},{3,11},{27,19},{4,12},{... | collective-permute-start | bytes 1007624 | tf_op jit(solution)/shard_map/ppermute | solution.py:210
  35.0 15.6 %collective-permute-start.3 = (f32[656,128]{1,0:T(8,128)S(1)}, f32[656,128]{1,0:T(8,128)S(1)}, u32[]{:S(2)}, u32[]{:S(2)}) collective-permute-start(f32[656,128]{1,0:T(8,128)S(1)} %collective-permute-done), channel_id=1, source_target_pairs={{8,24},{16,0},{9,25},{17,1},{10,26},{18,2},{11,27},{19,3},{12,28},... | collective-permute-start | bytes 1007624 | tf_op jit(solution)/shard_map/ppermute | solution.py:211
  52.9 10.1 %copy-start = (f32[10,256]{1,0:T(8,128)S(1)}, f32[10,256]{1,0:T(8,128)}, u32[]{:S(2)}) copy-start(f32[10,256]{1,0:T(8,128)} %get-tuple-element.42) | copy-start | bytes 30724
Sparse Core Ops, SparseCore 0:
  63.1 37.2 reduce-scatter.1

commit v3 on v2

--- a/solution.py
+++ b/solution.py
@@ -29,14 +29,16 @@
     return rows, columns
 
 
-def states_kernel(heads, width, x_ref, dy_ref, a_ref, b_ref, c_ref,
-                  xt_ref, dyt_ref, cum_ref, entry_ref, before_ref, packed_ref, sum_ref):
+def states_kernel(heads, width, role_ref, x_ref, dy_ref, a_ref, b_ref, c_ref,
+                  xt_ref, dyt_ref, cum_ref, entry_ref, before_ref, sendx_ref, sendy_ref,
+                  state_ref, adjoint_ref, sum_ref):
     k = pl.program_id(0)
     size = heads * width
 
     @pl.when(k == 0)
     def _():
-        packed_ref[...] = jnp.zeros_like(packed_ref)
+        state_ref[...] = jnp.zeros_like(state_ref)
+        adjoint_ref[...] = jnp.zeros_like(adjoint_ref)
         sum_ref[...] = jnp.zeros_like(sum_ref)
 
     x_t = x_ref[...].astype(F32).T
@@ -58,18 +60,23 @@
     own = mm(jnp.concatenate(weighted, axis=0), c_ref[...], NN)
     before = sum_ref[...]
     before_ref[0] = jnp.exp(before)
-    entry_ref[0] = packed_ref[:size]
-    for h in range(heads):
-        part = slice(h * width, (h + 1) * width)
-        later = slice(size + h * width, size + (h + 1) * width)
-        packed_ref[part] = packed_ref[part] * jnp.exp(last[h:h + 1]) + update[part]
-        packed_ref[later] = packed_ref[later] + jnp.exp(before[h:h + 1]) * own[part]
+    entry_ref[0] = state_ref[...]
+    for h in range(heads):
+        part = slice(h * width, (h + 1) * width)
+        state_ref[part] = state_ref[part] * jnp.exp(last[h:h + 1]) + update[part]
+        adjoint_ref[part] = adjoint_ref[part] + jnp.exp(before[h:h + 1]) * own[part]
     sum_ref[...] = before + last
-    packed_ref[2 * size:2 * size + heads] = before + last
-
-
-def local_kernel(heads, width, xt_ref, dyt_ref, cum_ref, b_ref, c_ref,
-                 inner_ref, back_ref, gain_ref, gbc_ref, skip_ref, gs_ref):
+
+    @pl.when(k == pl.num_programs(0) - 1)
+    def _():
+        for send_ref, place in ((sendx_ref, 0), (sendy_ref, 1)):
+            send_ref[:size] = jnp.where(role_ref[place] == 1, state_ref[...], adjoint_ref[...])
+            send_ref[size:] = jnp.zeros_like(send_ref[size:])
+            send_ref[size:size + heads] = before + last
+
+
+def local_kernel(heads, width, held, xt_ref, dyt_ref, cum_ref, b_ref, c_ref, *rest):
+    inner_ref, back_ref, gain_ref, gbc_ref, skip_ref, gs_ref = rest[held:]
     state_size = b_ref.shape[1]
 
     @pl.when(pl.program_id(0) == 0)
@@ -109,13 +116,35 @@
 
 
 def maps_kernel(heads, width, xt_ref, dyt_ref, cum_ref, c_ref, local_ref, before_ref,
-                entry_ref, after_ref, part_ref, gbc_ref, state_ref, adjoint_ref, edge_ref,
-                adj_ref, st_ref, scaled_ref, weighted_ref):
+                part_ref, role_ref, *rest):
+    received, rest = rest[:-9], rest[-9:]
+    (gbc_ref, state_ref, adjoint_ref, edge_ref,
+     adj_ref, st_ref, scaled_ref, weighted_ref, entry_ref) = rest
+    size = heads * width
     state_size = c_ref.shape[1]
 
     @pl.when(pl.program_id(0) == 0)
     def _():
-        adj_ref[...] = after_ref[...]
+        if len(received) == 2:
+            entry_ref[...] = received[0][...]
+            adj_ref[...] = received[1][...]
+            return
+        near_ref, side_ref, farx_ref, fary_ref = received
+        mine = role_ref[2]
+        for h in range(heads):
+            part = slice(h * width, (h + 1) * width)
+            row = slice(size + h, size + h + 1)
+            near, side = near_ref[part], side_ref[part]
+            far = farx_ref[part] + fary_ref[part]
+            near_sum, side_sum = near_ref[row], side_ref[row]
+            far_sum = farx_ref[row] + fary_ref[row]
+            whole = near + jnp.exp(near_sum) * side + jnp.exp(near_sum + side_sum) * far
+            double = far + jnp.exp(far_sum) * side
+            zero = jnp.zeros_like(near)
+            entry_ref[part] = jnp.where(
+                mine == 0, zero, jnp.where(mine == 1, near, jnp.where(mine == 2, double, whole)))
+            adj_ref[part] = jnp.where(
+                mine == 3, zero, jnp.where(mine == 2, near, jnp.where(mine == 1, double, whole)))
 
     cum = cum_ref[...]
     last = cum[:, SPAN - 1:]
@@ -178,9 +207,10 @@
     rate_ref[...] += grad * a_ref[...]
 
 
-def gathered(packed, heads, width, n):
+def gathered(state, adjoint, heads, width, n):
     size = heads * width
     count, mine = lax.axis_size("seq"), lax.axis_index("seq")
+    packed = jnp.concatenate([state[:size], adjoint], axis=0)
     pieces = lax.all_gather(packed, "seq")
     totals = pieces[:, 2 * size:2 * size + heads, 0]
     states = pieces[:, :size].reshape(count, heads, width, n)
@@ -198,28 +228,16 @@
     return entry, after
 
 
-def exchanged(packed, heads, width, n):
-    size = heads * width
-    mine = lax.axis_index("seq")
-    state = jnp.concatenate([packed[:size], packed[2 * size:]], axis=0)
-    adjoint = packed[size:]
-    by_x = lax.ppermute(jnp.where(mine % 2 == 0, state, adjoint), "seq",
-                        [(0, 1), (1, 0), (2, 3), (3, 2)])
-    by_y = lax.ppermute(jnp.where(mine < 2, state, adjoint), "seq",
-                        [(0, 2), (2, 0), (1, 3), (3, 1)])
-    far = (lax.ppermute(by_y, "seq", [(0, 1), (3, 2)])
-           + lax.ppermute(by_x, "seq", [(1, 3), (2, 0)]))
-
-    def cut(value):
-        return value[:size].reshape(heads, width, n), value[size:size + heads, :1, None]
-
-    (near, near_sum), (side, side_sum), (last, last_sum) = cut(by_x), cut(by_y), cut(far)
-    whole = near + jnp.exp(near_sum) * side + jnp.exp(near_sum + side_sum) * last
-    double = last + jnp.exp(last_sum) * side
-    zero = jnp.zeros_like(near)
-    entry = jnp.where(mine == 0, zero, jnp.where(mine == 1, near, jnp.where(mine == 2, double, whole)))
-    after = jnp.where(mine == 3, zero, jnp.where(mine == 2, near, jnp.where(mine == 1, double, whole)))
-    return entry.reshape(size, n), after.reshape(size, n)
+def first_round(send_x, send_y):
+    by_x = lax.ppermute(send_x, "seq", [(0, 1), (1, 0), (2, 3), (3, 2)])
+    by_y = lax.ppermute(send_y, "seq", [(0, 2), (2, 0), (1, 3), (3, 1)])
+    return by_x, by_y
+
+
+def second_round(by_x, by_y):
+    far_x = lax.ppermute(by_y, "seq", [(0, 1), (3, 2)])
+    far_y = lax.ppermute(by_x, "seq", [(1, 3), (2, 0)])
+    return far_x, far_y
 
 
 def shards(signal, log_decay, b_matrix, c_matrix, out_grad):
@@ -228,7 +246,15 @@
     width = size // heads
     n = b_matrix.shape[1]
     blocks = length // SPAN
-    padded = -(-(2 * size + heads) // 8) * 8
+    padded = -(-(size + heads) // 8) * 8
+    meshed = lax.axis_size("seq") == 4
+    mine = lax.axis_index("seq")
+    if meshed:
+        role = jnp.stack([mine % 2 == 0, mine < 2, mine]).astype(jnp.int32)
+    else:
+        role = jnp.array([1, 0, 0], jnp.int32)
+    scalars = pl.BlockSpec(memory_space=pltpu.SMEM)
+    anywhere = pl.BlockSpec(memory_space=pl.ANY)
     shape = jax.ShapeDtypeStruct
     params = pltpu.CompilerParams(vmem_limit_bytes=56 * 2**20)
 
@@ -236,62 +262,85 @@
     flat = pl.BlockSpec((size, SPAN), lambda k: (0, k))
     decay = pl.BlockSpec((heads, SPAN), lambda k: (0, k))
     maps = pl.BlockSpec((SPAN, n), lambda k: (k, 0))
-    xt, dyt, cum, local, before, packed = pl.pallas_call(
+    xt, dyt, cum, local, before, send_x, send_y = pl.pallas_call(
         functools.partial(states_kernel, heads, width),
         grid=(blocks,),
-        in_specs=[token, token, decay, maps, maps],
+        in_specs=[scalars, token, token, decay, maps, maps],
         out_specs=[flat, flat, decay,
                    pl.BlockSpec((1, size, n), lambda k: (k, 0, 0)),
                    pl.BlockSpec((1, heads, n), lambda k: (k, 0, 0)),
+                   pl.BlockSpec((padded, n), lambda k: (0, 0)),
                    pl.BlockSpec((padded, n), lambda k: (0, 0))],
         out_shape=[shape((size, length), BF16), shape((size, length), BF16),
                    shape((heads, length), F32), shape((blocks, size, n), F32),
-                   shape((blocks, heads, n), F32), shape((padded, n), F32)],
-        scratch_shapes=[pltpu.VMEM((heads, n), F32)],
+                   shape((blocks, heads, n), F32), shape((padded, n), F32),
+                   shape((padded, n), F32)],
+        scratch_shapes=[pltpu.VMEM((size, n), F32), pltpu.VMEM((size, n), F32),
+                        pltpu.VMEM((heads, n), F32)],
         compiler_params=params,
-    )(signal, out_grad, log_decay, b_matrix, c_matrix)
+    )(role, signal, out_grad, log_decay, b_matrix, c_matrix)
 
     def grad_cost(micros):
         return pl.CostEstimate(flops=int(micros * 1.0e9), bytes_accessed=int(micros * 3.0e6),
                                transcendentals=0)
 
     per_block = pl.BlockSpec((1, heads, n), lambda k: (k, 0, 0))
-    pair = pl.BlockSpec((SPAN, 2 * n), lambda k: (k, 0))
     once = pl.BlockSpec((heads, SPAN), lambda k: (0, 0))
-    inner, back, gain, local_maps, skip = pl.pallas_call(
-        functools.partial(local_kernel, heads, width),
-        grid=(blocks,),
-        in_specs=[flat, flat, decay, maps, maps],
-        out_specs=[flat, flat, decay, pair, once],
-        out_shape=[shape((size, length), F32), shape((size, length), F32),
-                   shape((heads, length), F32), shape((length, 2 * n), F32),
-                   shape((heads, SPAN), F32)],
-        scratch_shapes=[pltpu.VMEM((SPAN, SPAN), F32)],
-        compiler_params=params, cost_estimate=grad_cost(18),
-    )(xt, dyt, cum, b_matrix, c_matrix)
-
-    exchange = exchanged if lax.axis_size("seq") == 4 else gathered
-    entry, after = exchange(packed, heads, width, n)
+
+    def local_part(first, count, held):
+        def at(k):
+            return k + first
+
+        flat_at = pl.BlockSpec((size, SPAN), lambda k: (0, at(k)))
+        decay_at = pl.BlockSpec((heads, SPAN), lambda k: (0, at(k)))
+        maps_at = pl.BlockSpec((SPAN, n), lambda k: (at(k), 0))
+        pair_at = pl.BlockSpec((SPAN, 2 * n), lambda k: (at(k), 0))
+        return pl.pallas_call(
+            functools.partial(local_kernel, heads, width, len(held)),
+            grid=(count,),
+            in_specs=[flat_at, flat_at, decay_at, maps_at, maps_at] + [anywhere] * len(held),
+            out_specs=[flat_at, flat_at, decay_at, pair_at, once],
+            out_shape=[shape((size, length), F32), shape((size, length), F32),
+                       shape((heads, length), F32), shape((length, 2 * n), F32),
+                       shape((heads, SPAN), F32)],
+            scratch_shapes=[pltpu.VMEM((SPAN, SPAN), F32)],
+            input_output_aliases={5 + place: place for place in range(len(held))},
+            compiler_params=params, cost_estimate=grad_cost(2 * count),
+        )(xt, dyt, cum, b_matrix, c_matrix, *held)
+
+    half = blocks // 2
+    if meshed and half:
+        by_x, by_y = first_round(send_x, send_y)
+        *held, skip_first = local_part(0, half, [])
+        by_x, by_y, held = lax.optimization_barrier((by_x, by_y, held))
+        far_x, far_y = second_round(by_x, by_y)
+        inner, back, gain, local_maps, skip = local_part(half, blocks - half, held)
+        skip = skip + skip_first
+        received = (by_x, by_y, far_x, far_y)
+    else:
+        inner, back, gain, local_maps, skip = local_part(0, blocks, [])
+        received = gathered(send_x, send_y, heads, width, n)
 
     end = blocks - 1
     r_flat = pl.BlockSpec((size, SPAN), lambda k: (0, end - k))
     r_state = pl.BlockSpec((1, size, n), lambda k: (end - k, 0, 0))
     r_block = pl.BlockSpec((1, heads, n), lambda k: (end - k, 0, 0))
     r_pair = pl.BlockSpec((SPAN, 2 * n), lambda k: (end - k, 0))
-    edge_spec = pl.BlockSpec((size, n), lambda k: (0, 0))
+    whole_specs = [pl.BlockSpec(value.shape, lambda k: (0, 0)) for value in received]
     gbc, state_half, adj_half, edge = pl.pallas_call(
         functools.partial(maps_kernel, heads, width),
         grid=(blocks,),
         in_specs=[r_flat, r_flat, pl.BlockSpec((heads, SPAN), lambda k: (0, end - k)),
                   pl.BlockSpec((SPAN, n), lambda k: (end - k, 0)), r_state, r_block,
-                  edge_spec, edge_spec, r_pair],
+                  r_pair, scalars] + whole_specs,
         out_specs=[r_pair, r_state, r_state, r_block],
         out_shape=[shape((length, 2 * n), F32), shape((blocks, size, n), BF16),
                    shape((blocks, size, n), BF16), shape((blocks, heads, n), F32)],
         scratch_shapes=[pltpu.VMEM((size, n), F32), pltpu.VMEM((size, n), BF16),
-                        pltpu.VMEM((size, SPAN), BF16), pltpu.VMEM((size, SPAN), BF16)],
+                        pltpu.VMEM((size, SPAN), BF16), pltpu.VMEM((size, SPAN), BF16),
+                        pltpu.VMEM((size, n), F32)],
         compiler_params=params, cost_estimate=grad_cost(6),
-    )(xt, dyt, cum, c_matrix, local, before, entry, after, local_maps)
+    )(xt, dyt, cum, c_matrix, local, before, local_maps, role, *received)
 
     shared = lax.psum_scatter(gbc, "head", scatter_dimension=0, tiled=True)
 

time: 110 us -> 102 us (0.927)
  waiting for transfers between devices: 17.7 us -> 11.4 us
  Pallas kernels: 48.9 us -> 51.7 us
  other arithmetic: 4.11 us -> 1.54 us
  local copies, waits for them, and re-layouts: 3.93 us -> 2.52 us
  blocking collectives: 10.7 us -> 9.47 us
    ppermute x4, waiting for transfers between devices: 6.4 us -> 0.09 us  [the longest x1 0.08 us: first_round(): by_y = lax.ppermute(send_y, 'seq', [(0, 2), (2, 0), (1, 3), (3, 1)])]
    select_n x3 -> x0, other arithmetic: 2.98 us -> none  [the longest x1 1.06 us: exchanged(): jnp.where(mine == 3, zero, jnp.where(mine == 2, near, jnp.where(mine == 1...]
    pallas_call x1 -> x2, Pallas kernels: 13.9 us -> 15.9 us  [local_part(): pl.pallas_call(functools.partial(local_kernel, heads, width, len(held)),...]
    slice x2 -> x0, local copies, waits for them, and re-layouts: 1.7 us -> none  [exchanged(): state = jnp.concatenate([packed[:size], packed[2 * size:]], axis=0)]
    psum x1, blocking collectives: 10.7 us -> 9.47 us  [shards(): lax.psum(jnp.stack([jnp.sum(skip, axis=1), jnp.sum(rate, axis=1)]), 'seq')]
  transfers between devices with their start and end apart: 5 -> 5, of which waited for: 2 -> 2; matrix products, arithmetic and copies ran while one was open for 1% -> 1% of each run, Pallas kernels for 26% -> 30%
where the time goes in v3:
time: 102 us; the launch traced here: 101 us
  Pallas kernels  51.7 us (51%)
  between operations  14.2 us (14%)
  waiting for transfers between devices  11.4 us (11%)
  starting transfers between devices  10.4 us (10%)
  blocking collectives  9.47 us (9%)
  local copies, waits for them, and re-layouts  2.52 us (2%)
  other arithmetic  1.54 us (2%)
    pallas_call x2, Pallas kernels, local_part(): pl.pallas_call(functools.partial(local_kernel, heads, width, len(held)),...  15.9 us
    pallas_call x1, Pallas kernels, shards(): pl.pallas_call(functools.partial(output_kernel, heads, width), grid=(bloc...  14.4 us
    reduce_scatter x1, waiting for transfers between devices, shards(): shared = lax.psum_scatter(gbc, 'head', scatter_dimension=0, tiled=True)  11.3 us
    pallas_call x1, Pallas kernels, shards(): pl.pallas_call(functools.partial(states_kernel, heads, width), grid=(bloc...  11.3 us
    pallas_call x1, Pallas kernels, shards(): pl.pallas_call(functools.partial(maps_kernel, heads, width), grid=(blocks...  10.1 us
    psum x1, blocking collectives, shards(): lax.psum(jnp.stack([jnp.sum(skip, axis=1), jnp.sum(rate, axis=1)]), 'seq')  9.47 us
    ppermute x1, starting transfers between devices, second_round(): far_x = lax.ppermute(by_y, 'seq', [(0, 1), (3, 2)])  4.61 us
    ppermute x1, starting transfers between devices, first_round(): by_x = lax.ppermute(send_x, 'seq', [(0, 1), (1, 0), (2, 3), (3, 2)])  3 us
  transfers between devices with their start and end apart: 5, of which 2 were waited for; matrix products, arithmetic and copies ran while one was open for 1% of the time, Pallas kernels for 30%

profile of v3, /device:TPU:0, one launch (start us, length us, event | category | flops | bytes accessed | tf_op | source)
XLA Modules:
  0.0 101.3 jit_solution(2985808159790748052)
XLA Ops:
  7.2 0.0 reduce-scatter.2.cloned.1.call-start
  7.2 0.6 pad_add_fusion.role_ref
  7.8 11.3 %shard_map.100 = (bf16[640,2048]{1,0:T(8,128)(2,1)}, bf16[640,2048]{1,0:T(8,128)(2,1)}, f32[10,2048]{1,0:T(8,128)}, f32[8,640,128]{2,1,0:T(8,128)}, f32[8,10,128...) custom-call(s32[3]{0:T(128)} %pad_add_fusion.role_ref, bf16[2048,640]{1,0:T(8,128)(2,1)} %x_ref.1, ...), custom_call_target="tpu_custom_call" | custom-call | tf_op jit(solution)/shard_map/pallas_call | solution.py:265
  19.1 3.0 %collective-permute-start = (f32[656,128]{1,0:T(8,128)}, f32[656,128]{1,0:T(8,128)S(1)}, u32[]{:S(2)}, u32[]{:S(2)}) collective-permute-start(f32[656,128]{1,0:T(8,128)} %get-tuple-element.40), channel_id=1, source_target_pairs={{0,8},{8,0},{16,24},{24,16},{1,9},{9,1},{17,25},{25,17},{2,10},{10... | collective-permute-start | bytes 1007624 | tf_op jit(solution)/shard_map/ppermute | solution.py:232
  22.1 1.5 %collective-permute-start.1 = (f32[656,128]{1,0:T(8,128)}, f32[656,128]{1,0:T(8,128)S(1)}, u32[]{:S(2)}, u32[]{:S(2)}) collective-permute-start(f32[656,128]{1,0:T(8,128)} %get-tuple-element.41), channel_id=1, source_target_pairs={{0,16},{16,0},{8,24},{24,8},{1,17},{17,1},{9,25},{25,9},{2,18},{18... | collective-permute-start | bytes 1007624 | tf_op jit(solution)/shard_map/ppermute | solution.py:233
  23.6 7.9 %shard_map.101 = (f32[640,2048]{1,0:T(8,128)}, f32[640,2048]{1,0:T(8,128)}, f32[10,2048]{1,0:T(8,128)}, f32[2048,256]{1,0:T(8,128)}, f32[10,256]{1,0:T(8,128)}) custom-call(bf16[640,2048]{1,0:T(8,128)(2,1)} %get-tuple-element.37.xt_ref, bf16[640,2048]{1,0:T(8,128)(2,1)} %get-tuple-element.38.dyt_ref, f32[10,2048]{1,0:T(8,128)} %get-tuple-element.39.cum_ref, ...), custom_call_target="tpu_custom_call" | custom-call | flops 8000000000 | bytes 24000000 | tf_op jit(solution)/shard_map/pallas_call | solution.py:298
  31.6 0.0 collective-permute-done.rest_0_
  31.6 0.0 copy-start.2
  31.6 0.1 collective-permute-done.1.rest_1_
  31.7 0.0 copy-start.3
  31.7 1.3 %collective-permute-start.3 = (f32[656,128]{1,0:T(8,128)S(1)}, f32[656,128]{1,0:T(8,128)S(1)}, u32[]{:S(2)}, u32[]{:S(2)}) collective-permute-start(f32[656,128]{1,0:T(8,128)S(1)} %collective-permute-done.rest_0_), channel_id=1, source_target_pairs={{8,24},{16,0},{9,25},{17,1},{10,26},{18,2},{11,27},{19,3},{12,28},... | collective-permute-start | bytes 1007624 | tf_op jit(solution)/shard_map/ppermute | solution.py:239
  33.0 4.6 %collective-permute-start.2 = (f32[656,128]{1,0:T(8,128)S(1)}, f32[656,128]{1,0:T(8,128)S(1)}, u32[]{:S(2)}, u32[]{:S(2)}) collective-permute-start(f32[656,128]{1,0:T(8,128)S(1)} %collective-permute-done.1.rest_1_), channel_id=1, source_target_pairs={{0,8},{24,16},{1,9},{25,17},{2,10},{26,18},{3,11},{27,19},{4,12},{... | collective-permute-start | bytes 1007624 | tf_op jit(solution)/shard_map/ppermute | solution.py:238
  37.6 8.0 %shard_map.102 = (f32[640,2048]{1,0:T(8,128)}, f32[640,2048]{1,0:T(8,128)}, f32[10,2048]{1,0:T(8,128)}, f32[2048,256]{1,0:T(8,128)}, f32[10,256]{1,0:T(8,128)}) custom-call(bf16[640,2048]{1,0:T(8,128)(2,1)} %get-tuple-element.37.xt_ref, ...), custom_call_target="tpu_custom_call", output_to_operand_aliasing={{0}: (5, {}), {1}: (6, {}), {2}: (7, {}), {3}: (8, {})} | custom-call | flops 8000000000 | bytes 24000000 | tf_op jit(solution)/shard_map/pallas_call | solution.py:298
  45.6 0.0 copy-done.2
  45.6 0.0 copy-done.3
  45.6 0.0 collective-permute-done.3.rest_3_
  45.6 0.0 copy-start.4
  45.6 0.0 collective-permute-done.2.rest_2_
  45.6 0.0 copy-start.5
  45.6 0.7 copy-done.4
  46.3 0.1 copy-done.5
  46.4 0.0 copy-start
  46.4 0.0 copy-start.1
  46.4 10.1 %shard_map.103 = (f32[2048,256]{1,0:T(8,128)}, bf16[8,640,128]{2,1,0:T(8,128)(2,1)}, bf16[8,640,128]{2,1,0:T(8,128)(2,1)}, f32[8,10,128]{2,1,0:T(8,128)}) custom-call(bf16[640,2048]{1,0:T(8,128)(2,1)} %get-tuple-element.37.xt_ref, bf16[640,2048]{1,0:T(8,128)(2,1)} %get-tuple-element.38.dyt_ref, f32[10,2048]{1,0:T(8,128)} %get-tuple-element.39.cum_ref, ...), custom_call_target="tpu_custom_call" | custom-call | flops 6000000000 | bytes 18000000 | tf_op jit(solution)/shard_map/pallas_call | solution.py:330
  56.6 0.0 reduce-scatter.2.cloned.1.call-update
  56.6 0.0 copy-done
  56.6 0.0 copy-done.1
  56.6 0.1 add_reduce_fusion
  56.7 14.4 %shard_map.104 = (f32[2048,640]{1,0:T(8,128)}, f32[2048,640]{1,0:T(8,128)}, f32[10,2048]{1,0:T(8,128)}, f32[10,256]{1,0:T(8,128)}) custom-call(bf16[640,2048]{1,0:T(8,128)(2,1)} %get-tuple-element.37.xt_ref, bf16[640,2048]{1,0:T(8,128)(2,1)} %get-tuple-element.38.dyt_ref, f32[10,2048]{1,0:T(8,128)} %a_ref.3, f32[10,2048]{1,0:T(8,128)} %get-tuple-element.39.cum_ref, ...), custom_call_target="tpu_custom_call" | custom-call | flops 14000000000 | bytes 42000000 | tf_op jit(solution)/shard_map/pallas_call | solution.py:348
  71.1 0.8 reduce_sum.19
  72.0 9.5 %psum.7 = f32[2,10]{1,0:T(2,128)} all-reduce(f32[2,10]{1,0:T(2,128)S(1)} %pad_maximum_fusion), channel_id=1, replica_groups=mesh['seq'=4,'head'=8] {'seq'}, use_global_device_ids=true, to_apply=%region_3.4 | all-reduce | flops 20 | bytes 160 | tf_op jit(solution)/shard_map/psum | solution.py:360
  81.4 11.3 %reduce-scatter.2.cloned.1.call-done = f32[256,256]{1,0:T(8,128)} async-done(((f32[2048,256]{1,0:T(8,128)}), f32[256,256]{1,0:T(8,128)}) %reduce-scatter.2.cloned.1.call-update) | async-done | bytes 262160 | tf_op jit(solution)/shard_map/reduce_scatter | solution.py:345
  92.8 1.7 %fusion = (f32[256,128]{1,0:T(8,128)}, f32[256,128]{1,0:T(8,128)}) fusion(f32[256,256]{1,0:T(8,128)} %reduce-scatter.2.cloned.1.call-done), kind=kLoop, calls=%fused_computation.3 | loop fusion | bytes 524288 | tf_op jit(solution)/shard_map/slice | solution.py:361
  (1 shorter events, 0.0 us)
Async XLA Ops:
  7.2 85.6 %reduce-scatter.2.cloned.1.call-start = ((), (), s32[]{:S(2)}) async-start(), calls=%async_computation.1 | async-start | bytes 2359296 | tf_op jit(solution)/shard_map/reduce_scatter | solution.py:345
  19.1 12.5 %collective-permute-start = (f32[656,128]{1,0:T(8,128)}, f32[656,128]{1,0:T(8,128)S(1)}, u32[]{:S(2)}, u32[]{:S(2)}) collective-permute-start(f32[656,128]{1,0:T(8,128)} %get-tuple-element.40), channel_id=1, source_target_pairs={{0,8},{8,0},{16,24},{24,16},{1,9},{9,1},{17,25},{25,17},{2,10},{10... | collective-permute-start | bytes 1007624 | tf_op jit(solution)/shard_map/ppermute | solution.py:232
  22.1 9.6 %collective-permute-start.1 = (f32[656,128]{1,0:T(8,128)}, f32[656,128]{1,0:T(8,128)S(1)}, u32[]{:S(2)}, u32[]{:S(2)}) collective-permute-start(f32[656,128]{1,0:T(8,128)} %get-tuple-element.41), channel_id=1, source_target_pairs={{0,16},{16,0},{8,24},{24,8},{1,17},{17,1},{9,25},{25,9},{2,18},{18... | collective-permute-start | bytes 1007624 | tf_op jit(solution)/shard_map/ppermute | solution.py:233
  31.6 14.0 %copy-start.2 = (f32[656,128]{1,0:T(8,128)}, f32[656,128]{1,0:T(8,128)S(1)}, u32[]{:S(2)}) copy-start(f32[656,128]{1,0:T(8,128)S(1)} %collective-permute-done.rest_0_) | copy-start | bytes 1007620
  31.7 13.9 %copy-start.3 = (f32[656,128]{1,0:T(8,128)}, f32[656,128]{1,0:T(8,128)S(1)}, u32[]{:S(2)}) copy-start(f32[656,128]{1,0:T(8,128)S(1)} %collective-permute-done.1.rest_1_) | copy-start | bytes 1007620
  31.7 13.9 %collective-permute-start.3 = (f32[656,128]{1,0:T(8,128)S(1)}, f32[656,128]{1,0:T(8,128)S(1)}, u32[]{:S(2)}, u32[]{:S(2)}) collective-permute-start(f32[656,128]{1,0:T(8,128)S(1)} %collective-permute-done.rest_0_), channel_id=1, source_target_pairs={{8,24},{16,0},{9,25},{17,1},{10,26},{18,2},{11,27},{19,3},{12,28},... | collective-permute-start | bytes 1007624 | tf_op jit(solution)/shard_map/ppermute | solution.py:239
  33.0 12.6 %collective-permute-start.2 = (f32[656,128]{1,0:T(8,128)S(1)}, f32[656,128]{1,0:T(8,128)S(1)}, u32[]{:S(2)}, u32[]{:S(2)}) collective-permute-start(f32[656,128]{1,0:T(8,128)S(1)} %collective-permute-done.1.rest_1_), channel_id=1, source_target_pairs={{0,8},{24,16},{1,9},{25,17},{2,10},{26,18},{3,11},{27,19},{4,12},{... | collective-permute-start | bytes 1007624 | tf_op jit(solution)/shard_map/ppermute | solution.py:238
  45.6 0.8 copy-start.4
  45.6 0.8 copy-start.5
  46.4 10.2 %copy-start = (f32[10,256]{1,0:T(8,128)S(1)}, f32[10,256]{1,0:T(8,128)}, u32[]{:S(2)}) copy-start(f32[10,256]{1,0:T(8,128)} %get-tuple-element.66) | copy-start | bytes 30724
  46.4 10.2 %copy-start.1 = (f32[10,256]{1,0:T(8,128)S(1)}, f32[10,256]{1,0:T(8,128)}, u32[]{:S(2)}) copy-start(f32[10,256]{1,0:T(8,128)} %get-tuple-element.65) | copy-start | bytes 30724
Sparse Core Ops, SparseCore 0:
  56.7 35.9 reduce-scatter.1

commit v4 on v3

--- a/solution.py
+++ b/solution.py
@@ -117,8 +117,8 @@
 
 def maps_kernel(heads, width, xt_ref, dyt_ref, cum_ref, c_ref, local_ref, before_ref,
                 part_ref, role_ref, *rest):
-    received, rest = rest[:-9], rest[-9:]
-    (gbc_ref, state_ref, adjoint_ref, edge_ref,
+    received, rest = rest[:-8], rest[-8:]
+    (gbc_ref, state_ref, adjoint_ref,
      adj_ref, st_ref, scaled_ref, weighted_ref, entry_ref) = rest
     size = heads * width
     state_size = c_ref.shape[1]
@@ -152,22 +152,18 @@
     tail = jnp.exp(last - cum)
     whole = jnp.exp(last)
     before = before_ref[0]
-    edge = []
     for h in range(heads):
         part = slice(h * width, (h + 1) * width)
         state = local_ref[0, part] + before[h:h + 1] * entry_ref[part]
         st_ref[part] = state.astype(BF16)
-        products = jnp.sum(state * adj_ref[part], axis=0, keepdims=True)
-        edge.append(jnp.sum(products, axis=1, keepdims=True) * whole[h:h + 1])
         scaled_ref[part] = (xt_ref[part].astype(F32) * tail[h:h + 1]).astype(BF16)
         weighted_ref[part] = (dyt_ref[part].astype(F32) * head_decay[h:h + 1]).astype(BF16)
     state_half = st_ref[...]
     adj_half = adj_ref[...].astype(BF16)
     state_ref[0] = state_half
     adjoint_ref[0] = adj_half
-    edge_ref[0] = jnp.broadcast_to(jnp.concatenate(edge, axis=0), edge_ref.shape[1:])
-    gbc_ref[:, :state_size] = part_ref[:, :state_size] + mm(scaled_ref[...], adj_half, TN)
-    gbc_ref[:, state_size:] = part_ref[:, state_size:] + mm(weighted_ref[...], state_half, TN)
+    gbc_ref[:, :state_size] = part_ref[:, :state_size] + mm(adj_half, scaled_ref[...], TN).T
+    gbc_ref[:, state_size:] = part_ref[:, state_size:] + mm(state_half, weighted_ref[...], TN).T
     own = mm(weighted_ref[...], c_ref[...], NN)
     for h in range(heads):
         part = slice(h * width, (h + 1) * width)
@@ -175,7 +171,7 @@
 
 
 def output_kernel(heads, width, xt_ref, dyt_ref, a_ref, cum_ref, b_ref, c_ref, inner_ref, back_ref,
-                  gain_ref, state_ref, adjoint_ref, edge_ref,
+                  gain_ref, state_ref, adjoint_ref,
                   y_ref, gx_ref, ga_ref, rate_ref, yt_ref, gxt_ref):
     @pl.when(pl.program_id(0) == 0)
     def _():
@@ -188,7 +184,7 @@
     tail = jnp.exp(last - cum)
     carried_all = mm(state_ref[0], c_ref[...], NT)
     scaled_grad_all = mm(adjoint_ref[0], b_ref[...], NT)
-    gain, loss = [], []
+    gain, loss, edge = [], [], []
     for h in range(heads):
         part = slice(h * width, (h + 1) * width)
         x, dy = xt_ref[part].astype(F32), dyt_ref[part].astype(F32)
@@ -198,11 +194,13 @@
         gxt_ref[part] = back_ref[part] + tailed + dy
         gain.append(jnp.sum(dy * carried, axis=0, keepdims=True))
         loss.append(jnp.sum(x * tailed, axis=0, keepdims=True))
+        edge.append(jnp.sum(state_ref[0, part].astype(F32) * adjoint_ref[0, part].astype(F32),
+                            axis=0, keepdims=True))
     y_ref[...] = yt_ref[...].T
     gx_ref[...] = gxt_ref[...].T
     grad = (sums(gain_ref[...] + jnp.concatenate(gain, axis=0), (rows >= columns).astype(F32))
             + sums(jnp.concatenate(loss, axis=0), (rows < columns).astype(F32))
-            + edge_ref[0][:, :1])
+            + jnp.exp(last) * jnp.sum(jnp.concatenate(edge, axis=0), axis=1, keepdims=True))
     ga_ref[...] = grad
     rate_ref[...] += grad * a_ref[...]
 
@@ -284,7 +282,6 @@
         return pl.CostEstimate(flops=int(micros * 1.0e9), bytes_accessed=int(micros * 3.0e6),
                                transcendentals=0)
 
-    per_block = pl.BlockSpec((1, heads, n), lambda k: (k, 0, 0))
     once = pl.BlockSpec((heads, SPAN), lambda k: (0, 0))
 
     def local_part(first, count, held):
@@ -327,15 +324,15 @@
     r_block = pl.BlockSpec((1, heads, n), lambda k: (end - k, 0, 0))
     r_pair = pl.BlockSpec((SPAN, 2 * n), lambda k: (end - k, 0))
     whole_specs = [pl.BlockSpec(value.shape, lambda k: (0, 0)) for value in received]
-    gbc, state_half, adj_half, edge = pl.pallas_call(
+    gbc, state_half, adj_half = pl.pallas_call(
         functools.partial(maps_kernel, heads, width),
         grid=(blocks,),
         in_specs=[r_flat, r_flat, pl.BlockSpec((heads, SPAN), lambda k: (0, end - k)),
                   pl.BlockSpec((SPAN, n), lambda k: (end - k, 0)), r_state, r_block,
                   r_pair, scalars] + whole_specs,
-        out_specs=[r_pair, r_state, r_state, r_block],
+        out_specs=[r_pair, r_state, r_state],
         out_shape=[shape((length, 2 * n), F32), shape((blocks, size, n), BF16),
-                   shape((blocks, size, n), BF16), shape((blocks, heads, n), F32)],
+                   shape((blocks, size, n), BF16)],
         scratch_shapes=[pltpu.VMEM((size, n), F32), pltpu.VMEM((size, n), BF16),
                         pltpu.VMEM((size, SPAN), BF16), pltpu.VMEM((size, SPAN), BF16),
                         pltpu.VMEM((size, n), F32)],
@@ -349,13 +346,13 @@
         functools.partial(output_kernel, heads, width),
         grid=(blocks,),
         in_specs=[flat, flat, decay, decay, maps, maps, flat, flat, decay,
-                  state_spec, state_spec, per_block],
+                  state_spec, state_spec],
         out_specs=[token, token, decay, once],
         out_shape=[shape((length, size), F32), shape((length, size), F32),
                    shape((heads, length), F32), shape((heads, SPAN), F32)],
         scratch_shapes=[pltpu.VMEM((size, SPAN), F32), pltpu.VMEM((size, SPAN), F32)],
         compiler_params=params, cost_estimate=grad_cost(14),
-    )(xt, dyt, log_decay, cum, b_matrix, c_matrix, inner, back, gain, state_half, adj_half, edge)
+    )(xt, dyt, log_decay, cum, b_matrix, c_matrix, inner, back, gain, state_half, adj_half)
 
     head_grads = lax.psum(jnp.stack([jnp.sum(skip, axis=1), jnp.sum(rate, axis=1)]), "seq")
     return y, gx, ga, shared[:, :n], shared[:, n:], head_grads

time: 102 us -> 102 us (level)
  no operation moved by 1% of the time
where the time goes in v4:
time: 102 us; the launch traced here: 101 us
  Pallas kernels  51.9 us (51%)
  between operations  14.2 us (14%)
  waiting for transfers between devices  11.4 us (11%)
  starting transfers between devices  10.5 us (10%)
  blocking collectives  9.46 us (9%)
  local copies, waits for them, and re-layouts  2.52 us (2%)
  other arithmetic  1.56 us (2%)
    pallas_call x2, Pallas kernels, local_part(): pl.pallas_call(functools.partial(local_kernel, heads, width, len(held)),...  15.9 us
    pallas_call x1, Pallas kernels, shards(): pl.pallas_call(functools.partial(output_kernel, heads, width), grid=(bloc...  14.4 us
    reduce_scatter x1, waiting for transfers between devices, shards(): shared = lax.psum_scatter(gbc, 'head', scatter_dimension=0, tiled=True)  11.3 us
    pallas_call x1, Pallas kernels, shards(): pl.pallas_call(functools.partial(states_kernel, heads, width), grid=(bloc...  11.3 us
    pallas_call x1, Pallas kernels, shards(): pl.pallas_call(functools.partial(maps_kernel, heads, width), grid=(blocks...  10.3 us
    psum x1, blocking collectives, shards(): lax.psum(jnp.stack([jnp.sum(skip, axis=1), jnp.sum(rate, axis=1)]), 'seq')  9.46 us
    ppermute x1, starting transfers between devices, second_round(): far_x = lax.ppermute(by_y, 'seq', [(0, 1), (3, 2)])  4.61 us
    ppermute x1, starting transfers between devices, first_round(): by_x = lax.ppermute(send_x, 'seq', [(0, 1), (1, 0), (2, 3), (3, 2)])  3.01 us
  transfers between devices with their start and end apart: 5, of which 2 were waited for; matrix products, arithmetic and copies ran while one was open for 1% of the time, Pallas kernels for 30%

profile of v4, /device:TPU:0, one launch (start us, length us, event | category | flops | bytes accessed | tf_op | source)
XLA Modules:
  0.0 101.5 jit_solution(6674309445169925912)
XLA Ops:
  7.2 0.0 reduce-scatter.2.cloned.1.call-start
  7.2 0.6 pad_add_fusion.role_ref
  7.8 11.3 %shard_map.100 = (bf16[640,2048]{1,0:T(8,128)(2,1)}, bf16[640,2048]{1,0:T(8,128)(2,1)}, f32[10,2048]{1,0:T(8,128)}, f32[8,640,128]{2,1,0:T(8,128)}, f32[8,10,128...) custom-call(s32[3]{0:T(128)} %pad_add_fusion.role_ref, bf16[2048,640]{1,0:T(8,128)(2,1)} %x_ref.1, ...), custom_call_target="tpu_custom_call" | custom-call | tf_op jit(solution)/shard_map/pallas_call | solution.py:263
  19.1 3.0 %collective-permute-start = (f32[656,128]{1,0:T(8,128)}, f32[656,128]{1,0:T(8,128)S(1)}, u32[]{:S(2)}, u32[]{:S(2)}) collective-permute-start(f32[656,128]{1,0:T(8,128)} %get-tuple-element.39), channel_id=1, source_target_pairs={{0,8},{8,0},{16,24},{24,16},{1,9},{9,1},{17,25},{25,17},{2,10},{10... | collective-permute-start | bytes 1007624 | tf_op jit(solution)/shard_map/ppermute | solution.py:230
  22.1 1.5 %collective-permute-start.1 = (f32[656,128]{1,0:T(8,128)}, f32[656,128]{1,0:T(8,128)S(1)}, u32[]{:S(2)}, u32[]{:S(2)}) collective-permute-start(f32[656,128]{1,0:T(8,128)} %get-tuple-element.40), channel_id=1, source_target_pairs={{0,16},{16,0},{8,24},{24,8},{1,17},{17,1},{9,25},{25,9},{2,18},{18... | collective-permute-start | bytes 1007624 | tf_op jit(solution)/shard_map/ppermute | solution.py:231
  23.7 7.9 %shard_map.101 = (f32[640,2048]{1,0:T(8,128)}, f32[640,2048]{1,0:T(8,128)}, f32[10,2048]{1,0:T(8,128)}, f32[2048,256]{1,0:T(8,128)}, f32[10,256]{1,0:T(8,128)}) custom-call(bf16[640,2048]{1,0:T(8,128)(2,1)} %get-tuple-element.36.xt_ref, bf16[640,2048]{1,0:T(8,128)(2,1)} %get-tuple-element.37.dyt_ref, f32[10,2048]{1,0:T(8,128)} %get-tuple-element.38.cum_ref, ...), custom_call_target="tpu_custom_call" | custom-call | flops 8000000000 | bytes 24000000 | tf_op jit(solution)/shard_map/pallas_call | solution.py:295
  31.6 0.0 collective-permute-done.rest_0_
  31.6 0.0 copy-start.2
  31.6 0.1 collective-permute-done.1.rest_1_
  31.7 0.0 copy-start.3
  31.7 1.3 %collective-permute-start.3 = (f32[656,128]{1,0:T(8,128)S(1)}, f32[656,128]{1,0:T(8,128)S(1)}, u32[]{:S(2)}, u32[]{:S(2)}) collective-permute-start(f32[656,128]{1,0:T(8,128)S(1)} %collective-permute-done.rest_0_), channel_id=1, source_target_pairs={{8,24},{16,0},{9,25},{17,1},{10,26},{18,2},{11,27},{19,3},{12,28},... | collective-permute-start | bytes 1007624 | tf_op jit(solution)/shard_map/ppermute | solution.py:237
  33.0 4.6 %collective-permute-start.2 = (f32[656,128]{1,0:T(8,128)S(1)}, f32[656,128]{1,0:T(8,128)S(1)}, u32[]{:S(2)}, u32[]{:S(2)}) collective-permute-start(f32[656,128]{1,0:T(8,128)S(1)} %collective-permute-done.1.rest_1_), channel_id=1, source_target_pairs={{0,8},{24,16},{1,9},{25,17},{2,10},{26,18},{3,11},{27,19},{4,12},{... | collective-permute-start | bytes 1007624 | tf_op jit(solution)/shard_map/ppermute | solution.py:236
  37.6 8.0 %shard_map.102 = (f32[640,2048]{1,0:T(8,128)}, f32[640,2048]{1,0:T(8,128)}, f32[10,2048]{1,0:T(8,128)}, f32[2048,256]{1,0:T(8,128)}, f32[10,256]{1,0:T(8,128)}) custom-call(bf16[640,2048]{1,0:T(8,128)(2,1)} %get-tuple-element.36.xt_ref, ...), custom_call_target="tpu_custom_call", output_to_operand_aliasing={{0}: (5, {}), {1}: (6, {}), {2}: (7, {}), {3}: (8, {})} | custom-call | flops 8000000000 | bytes 24000000 | tf_op jit(solution)/shard_map/pallas_call | solution.py:295
  45.6 0.0 copy-done.2
  45.6 0.0 copy-done.3
  45.6 0.0 collective-permute-done.3.rest_3_
  45.6 0.0 copy-start.4
  45.6 0.0 collective-permute-done.2.rest_2_
  45.6 0.0 copy-start.5
  45.6 0.7 copy-done.4
  46.4 0.1 copy-done.5
  46.5 0.0 copy-start
  46.5 0.0 copy-start.1
  46.5 10.3 %shard_map.103 = (f32[2048,256]{1,0:T(8,128)}, bf16[8,640,128]{2,1,0:T(8,128)(2,1)}, bf16[8,640,128]{2,1,0:T(8,128)(2,1)}) custom-call(bf16[640,2048]{1,0:T(8,128)(2,1)} %get-tuple-element.36.xt_ref, bf16[640,2048]{1,0:T(8,128)(2,1)} %get-tuple-element.37.dyt_ref, f32[10,2048]{1,0:T(8,128)} %get-tuple-element.38.cum_ref, bf16[2048,128]{1,0:T(8,128)(2,1)} %c_ref.9, ...), custom_call_target="tpu_custom_call" | custom-call | flops 6000000000 | bytes 18000000 | tf_op jit(solution)/shard_map/pallas_call | solution.py:327
  56.8 0.0 reduce-scatter.2.cloned.1.call-update
  56.8 0.0 copy-done
  56.8 0.0 copy-done.1
  56.8 0.1 add_reduce_fusion
  57.0 14.4 %shard_map.104 = (f32[2048,640]{1,0:T(8,128)}, f32[2048,640]{1,0:T(8,128)}, f32[10,2048]{1,0:T(8,128)}, f32[10,256]{1,0:T(8,128)}) custom-call(bf16[640,2048]{1,0:T(8,128)(2,1)} %get-tuple-element.36.xt_ref, bf16[640,2048]{1,0:T(8,128)(2,1)} %get-tuple-element.37.dyt_ref, f32[10,2048]{1,0:T(8,128)} %a_ref.3, f32[10,2048]{1,0:T(8,128)} %get-tuple-element.38.cum_ref, ...), custom_call_target="tpu_custom_call" | custom-call | flops 14000000000 | bytes 42000000 | tf_op jit(solution)/shard_map/pallas_call | solution.py:345
  71.3 0.8 reduce_sum.19
  72.2 9.5 %psum.7 = f32[2,10]{1,0:T(2,128)} all-reduce(f32[2,10]{1,0:T(2,128)S(1)} %pad_maximum_fusion), channel_id=1, replica_groups=mesh['seq'=4,'head'=8] {'seq'}, use_global_device_ids=true, to_apply=%region_3.4 | all-reduce | flops 20 | bytes 160 | tf_op jit(solution)/shard_map/psum | solution.py:357
  81.6 11.3 %reduce-scatter.2.cloned.1.call-done = f32[256,256]{1,0:T(8,128)} async-done(((f32[2048,256]{1,0:T(8,128)}), f32[256,256]{1,0:T(8,128)}) %reduce-scatter.2.cloned.1.call-update) | async-done | bytes 262160 | tf_op jit(solution)/shard_map/reduce_scatter | solution.py:342
  93.0 1.7 %fusion = (f32[256,128]{1,0:T(8,128)}, f32[256,128]{1,0:T(8,128)}) fusion(f32[256,256]{1,0:T(8,128)} %reduce-scatter.2.cloned.1.call-done), kind=kLoop, calls=%fused_computation.3 | loop fusion | bytes 524288 | tf_op jit(solution)/shard_map/slice | solution.py:358
  (1 shorter events, 0.0 us)
Async XLA Ops:
  7.2 85.8 %reduce-scatter.2.cloned.1.call-start = ((), (), s32[]{:S(2)}) async-start(), calls=%async_computation.1 | async-start | bytes 2359296 | tf_op jit(solution)/shard_map/reduce_scatter | solution.py:342
  19.1 12.5 %collective-permute-start = (f32[656,128]{1,0:T(8,128)}, f32[656,128]{1,0:T(8,128)S(1)}, u32[]{:S(2)}, u32[]{:S(2)}) collective-permute-start(f32[656,128]{1,0:T(8,128)} %get-tuple-element.39), channel_id=1, source_target_pairs={{0,8},{8,0},{16,24},{24,16},{1,9},{9,1},{17,25},{25,17},{2,10},{10... | collective-permute-start | bytes 1007624 | tf_op jit(solution)/shard_map/ppermute | solution.py:230
  22.1 9.6 %collective-permute-start.1 = (f32[656,128]{1,0:T(8,128)}, f32[656,128]{1,0:T(8,128)S(1)}, u32[]{:S(2)}, u32[]{:S(2)}) collective-permute-start(f32[656,128]{1,0:T(8,128)} %get-tuple-element.40), channel_id=1, source_target_pairs={{0,16},{16,0},{8,24},{24,8},{1,17},{17,1},{9,25},{25,9},{2,18},{18... | collective-permute-start | bytes 1007624 | tf_op jit(solution)/shard_map/ppermute | solution.py:231
  31.6 14.0 %copy-start.2 = (f32[656,128]{1,0:T(8,128)}, f32[656,128]{1,0:T(8,128)S(1)}, u32[]{:S(2)}) copy-start(f32[656,128]{1,0:T(8,128)S(1)} %collective-permute-done.rest_0_) | copy-start | bytes 1007620
  31.7 13.9 %copy-start.3 = (f32[656,128]{1,0:T(8,128)}, f32[656,128]{1,0:T(8,128)S(1)}, u32[]{:S(2)}) copy-start(f32[656,128]{1,0:T(8,128)S(1)} %collective-permute-done.1.rest_1_) | copy-start | bytes 1007620
  31.7 13.9 %collective-permute-start.3 = (f32[656,128]{1,0:T(8,128)S(1)}, f32[656,128]{1,0:T(8,128)S(1)}, u32[]{:S(2)}, u32[]{:S(2)}) collective-permute-start(f32[656,128]{1,0:T(8,128)S(1)} %collective-permute-done.rest_0_), channel_id=1, source_target_pairs={{8,24},{16,0},{9,25},{17,1},{10,26},{18,2},{11,27},{19,3},{12,28},... | collective-permute-start | bytes 1007624 | tf_op jit(solution)/shard_map/ppermute | solution.py:237
  33.0 12.6 %collective-permute-start.2 = (f32[656,128]{1,0:T(8,128)S(1)}, f32[656,128]{1,0:T(8,128)S(1)}, u32[]{:S(2)}, u32[]{:S(2)}) collective-permute-start(f32[656,128]{1,0:T(8,128)S(1)} %collective-permute-done.1.rest_1_), channel_id=1, source_target_pairs={{0,8},{24,16},{1,9},{25,17},{2,10},{26,18},{3,11},{27,19},{4,12},{... | collective-permute-start | bytes 1007624 | tf_op jit(solution)/shard_map/ppermute | solution.py:236
  45.6 0.8 copy-start.4
  45.6 0.8 copy-start.5
  46.5 10.4 %copy-start = (f32[10,256]{1,0:T(8,128)S(1)}, f32[10,256]{1,0:T(8,128)}, u32[]{:S(2)}) copy-start(f32[10,256]{1,0:T(8,128)} %get-tuple-element.64) | copy-start | bytes 30724
  46.5 10.4 %copy-start.1 = (f32[10,256]{1,0:T(8,128)S(1)}, f32[10,256]{1,0:T(8,128)}, u32[]{:S(2)}) copy-start(f32[10,256]{1,0:T(8,128)} %get-tuple-element.63) | copy-start | bytes 30724
Sparse Core Ops, SparseCore 0:
  56.9 35.9 reduce-scatter.1
